TPU v7x, 128 devices: a whole 4x4x4 slice. The times are simulated.
128 devices in a mesh: row: 8 (over x, core), col: 16 (over y, z).
Axes of the slice: x: 4, y: 4, z: 4, core: 2. Of those that a mesh axis runs over, the one named last changes fastest.
Arguments:
- orbitals: float32 [512, 32, 1024], P(('row', 'col')), may hold values from -6 to 6
- gradient: float32 [512, 32, 1024], P(('row', 'col')), may hold values from -4 to 4
- offsets: int32 [512, 3], replicated, may hold values from 0 to 3
- pairs: int32 [128, 4, 2], P('row'), may hold values from 0 to 511, as said below
- counts: int32 [128], P('row'), may hold values from 1 to 4, as said below
Outputs:
- updated: float32 [512, 32, 1024], P(('row', 'col'))
- energies: float32 [2], replicated
Inputs may be any that keep to these rules, and one draw needn't show every extreme that they name: `pairs`: both orbitals of a slot of pair owner p belong to p's group, ids g * 64 to (g + 1) * 64 - 1 with g = p // 16 (device d owns ids d * 4 onward). Among the live slots of one pair owner at most 2 distinct orbitals come from any one device, and every owner reaches 2 from some device. `counts`: every group of 16 pair owners has one owner with 4 live slots.
All inputs are finite; a program needn't handle non-finite values.
Results may differ from a plain program's by a relative error of at most 0.0082.
Values may be sent and summed in bfloat16 or wider, within the bound.
A program may use at most 64 MiB of HBM per device.

v0:
```python
import jax
import jax.numpy as jnp
from jax import lax
from jax.sharding import Mesh
from jax.sharding import PartitionSpec as P

CAP = 2
SHIFT = 4
SWEEPS = 12
ROUNDS = 2
COL = ("col_0", "col_1")
ROW = ("row_0", "row_1")
ROW_COL = ("row_0", "row_1", "col_0", "col_1")


screen_mu = 0.1
damping = 0.5


def by_axis(x, axes):
    for axis in axes:
        x = lax.psum(x, axis)
    return x


def sweep_table(sweeps):
    center_val = 6.0 + screen_mu
    half_width = 6.0
    ratio_val = center_val / half_width
    prev_coef = 1.0 / ratio_val
    keep_list = []
    mix_list = []
    for sweep_idx in range(sweeps):
        next_coef = 1.0 / (2.0 * ratio_val - prev_coef)
        keep_list.append(next_coef * prev_coef)
        mix_list.append(2.0 * next_coef / half_width)
        prev_coef = next_coef
    return (jnp.array(keep_list, jnp.float32), jnp.array(mix_list, jnp.float32), 1.0 / center_val)


def apply_operator(field):
    edge = field.shape[0]
    plane = field.shape[1]
    zero_row = jnp.zeros_like(field[:1])
    along_x = jnp.concatenate([field[1:], zero_row], 0) + jnp.concatenate([zero_row, field[:-1]], 0)
    zero_band = jnp.zeros_like(field[:, :edge])
    along_y = jnp.concatenate([field[:, edge:], zero_band], 1) + jnp.concatenate(
        [zero_band, field[:, :-edge]], 1
    )
    zero_col = jnp.zeros_like(field[:, :1])
    depth = jnp.arange(plane) % edge
    upper = jnp.where(depth < edge - 1, jnp.concatenate([field[:, 1:], zero_col], 1), 0.0)
    lower = jnp.where(depth > 0, jnp.concatenate([zero_col, field[:, :-1]], 1), 0.0)
    return (6.0 + screen_mu) * field - (along_x + along_y + upper + lower)


def screened_solve(source, tables):
    keep_coef, mix_coef, first_coef = tables

    def sweep(index, state):
        solution, remainder, direction = state
        solution = solution + direction
        remainder = remainder - apply_operator(direction)
        direction = keep_coef[index] * direction + mix_coef[index] * remainder
        return (solution, remainder, direction)

    state = (jnp.zeros_like(source), source, source * first_coef)
    return lax.fori_loop(0, keep_coef.shape[0], sweep, state)[0]


def displaced(box, shift):
    edge = box.shape[0]
    reach = SHIFT - 1
    cube = jnp.pad(box.reshape(edge, edge, edge), reach)
    start = shift + reach
    moved = lax.dynamic_slice(cube, (start[0], start[1], start[2]), (edge, edge, edge))
    return moved.reshape(edge, edge * edge)


def run_pairs(boxes, source_of, slot_of, mine, mine_count, group_offsets, tables, slots):
    edge = boxes.shape[1]
    plane = boxes.shape[2]
    collected = jnp.zeros((slots, edge, plane), jnp.float32)

    def one_pair(index, state):
        gathered, energy = state
        first = mine[index, 0]
        second = mine[index, 1]
        shift = group_offsets[first] - group_offsets[second]
        box_i = lax.dynamic_index_in_dim(boxes, source_of[first], 0, False).astype(jnp.float32)
        box_j = displaced(
            lax.dynamic_index_in_dim(boxes, source_of[second], 0, False), shift
        ).astype(jnp.float32)
        density = box_i * box_j
        potential = screened_solve(density, tables)
        term = potential * box_j
        target = slot_of[first]
        current = lax.dynamic_index_in_dim(gathered, target, 0, False)
        gathered = lax.dynamic_update_index_in_dim(gathered, current + term, target, 0)
        return (gathered, energy + jnp.sum(density * potential))

    return lax.fori_loop(0, mine_count, one_pair, (collected, jnp.zeros((), jnp.float32)))


def local(orbitals, gradient, offsets, pairs, counts):
    tables = sweep_table(SWEEPS)
    own_count = orbitals.shape[0]
    edge = orbitals.shape[1]
    plane = orbitals.shape[2]
    columns = lax.axis_size(COL)
    own_index = lax.axis_index(COL)
    group = columns * own_count
    slots = columns * CAP
    base = lax.axis_index(ROW) * group
    local_pairs = pairs - base
    group_offsets = lax.dynamic_slice_in_dim(offsets, base, group, 0)
    orbit_ids = jnp.arange(group, dtype=jnp.int32)
    live = jnp.arange(local_pairs.shape[1])[None, :] < counts[:, None]
    hits = (local_pairs[:, :, 0, None] == orbit_ids) | (local_pairs[:, :, 1, None] == orbit_ids)
    needed = (
        jnp.any(hits & live[:, :, None], axis=1)
        .astype(jnp.int32)
        .reshape(columns, columns, own_count)
    )
    ranks = jnp.cumsum(needed, axis=2) - 1
    send_need = lax.dynamic_index_in_dim(needed, own_index, 1, False)
    send_rank = lax.dynamic_index_in_dim(ranks, own_index, 1, False)
    slot_ids = jnp.arange(CAP)
    plan = (
        (send_need[:, None, :] == 1) & (send_rank[:, None, :] == slot_ids[None, :, None])
    ).astype(jnp.bfloat16)
    recv_rank = lax.dynamic_index_in_dim(ranks, own_index, 0, False)
    slot_of = (jnp.arange(columns)[:, None] * CAP + recv_rank).reshape(group)
    mine = lax.dynamic_index_in_dim(local_pairs, own_index, 0, False)
    mine_count = lax.dynamic_index_in_dim(counts, own_index, 0, False)
    current = orbitals
    totals = []
    for round_idx in range(ROUNDS):
        boxes_own = current.astype(jnp.bfloat16)
        outgoing = jnp.einsum(
            "pkm,mc->pkc",
            plan,
            boxes_own.reshape(own_count, edge * plane),
            preferred_element_type=jnp.float32,
        ).astype(jnp.bfloat16)
        arrived = lax.all_to_all(outgoing, COL, split_axis=0, concat_axis=0, tiled=True).reshape(
            slots, edge, plane
        )
        gathered, energy = run_pairs(
            arrived, slot_of, slot_of, mine, mine_count, group_offsets, tables, slots
        )
        slot_terms = gathered.astype(jnp.bfloat16).reshape(columns, CAP, edge * plane)
        returned = lax.all_to_all(slot_terms, COL, split_axis=0, concat_axis=0, tiled=True)
        exchange_term = jnp.einsum(
            "pkm,pkc->mc", plan, returned, preferred_element_type=jnp.float32
        )
        current = current - damping * (gradient + exchange_term.reshape(own_count, edge, plane))
        totals.append(energy)
    summed = by_axis(jnp.stack(totals), ROW_COL)
    energies = summed / (edge * edge * edge * lax.axis_size(ROW) * columns)
    return (current, energies)


def solution(mesh):
    finer = Mesh(mesh.devices.reshape(4, 2, 4, 4), ("row_0", "row_1", "col_0", "col_1"))
    in_specs = (P(ROW_COL, None, None), P(ROW_COL, None, None), P(), P(ROW, None, None), P(ROW))
    out_specs = (P(ROW_COL, None, None), P())
    return jax.shard_map(local, mesh=finer, in_specs=in_specs, out_specs=out_specs, check_vma=False)
```

profile of v0, /device:TPU:1, one launch (start us, length us, event | category | flops | bytes accessed | tf_op | source)
XLA Modules:
  0.0 644.5 jit_solution(5633085483786422583)
XLA Ops:
  4.4 3.5 copy.30
  7.9 8.7 %all-to-all-start = ((bf16[16,2,32768]{2,1,0:T(2,128)(2,1)}), bf16[16,2,32768]{2,1,0:T(2,128)(2,1)S(1)}, u32[]{:S(2)}, u32[]{:S(2)}) async-start(bf16[16,2,32768]{2,1,0:T(2,128)(2,1)} %copy.30), calls=%async_computation | async-start | bytes 4194304 | tf_op jit(solution)/shard_map/all_to_all | solution.py:146
  18.2 26.3 %all-to-all-done = bf16[16,2,32768]{2,1,0:T(2,128)(2,1)S(1)} async-done(((bf16[16,2,32768]{2,1,0:T(2,128)(2,1)}), bf16[16,2,32768]{2,1,0:T(2,128)(2,1)S(1)}, u32[]{:S(2)}, u32[]{:S(2)}) %all-to-all-start) | async-done | bytes 2097184 | tf_op jit(solution)/shard_map/all_to_all | solution.py:146
  44.5 2.8 reshape.110
  49.8 117.9 %while.91 = (s32[]{:T(128)}, f32[32,32,1024]{2,1,0:T(8,128)}, f32[]{:T(128)}, s32[]{:T(128)}, s32[4,2]{0,1:T(2,128)S(1)}, /*index=5*/s32[64]{0:T(128)S(1)}, bf16...) while((s32[]{:T(128)}, f32[32,32,1024]{2,1,0:T(8,128)}, ...), condition=%wide.region_6.7_spmd.clone, body=%wide.region_2.6_spmd.sunk.clone.sunk | while | flops 761891 | bytes 5591096 | solution.py:102
  69.5 36.9 %while.94 = (s32[]{:T(128)}, f32[32,1024]{1,0:T(8,128)S(1)}, f32[32,1024]{1,0:T(8,128)S(1)}, f32[32,1024]{1,0:T(8,128)S(1)}, s32[]{:T(128)}, /*index=5*/f32[12]{0:T(128)S(1)}, f32[12]{0:T(128)S(1)}, s32[]{:T(128)}) while((s32[]{:T(128)}, f32[32,1024]{1,0:T(8,128)S(1)}, f32[32,1024]{1,0:T(8,128)S(1)}, ...), condition=%wide.region_4.4_spmd.clone.clone, body=%wide.region_3.3_spmd.sunk.clone.clone.sunk | while | flops 499715 | bytes 3100039 | solution.py:68
  128.1 36.9 %while.94 = (s32[]{:T(128)}, f32[32,1024]{1,0:T(8,128)S(1)}, f32[32,1024]{1,0:T(8,128)S(1)}, f32[32,1024]{1,0:T(8,128)S(1)}, s32[]{:T(128)}, /*index=5*/f32[12]{0:T(128)S(1)}, f32[12]{0:T(128)S(1)}, s32[]{:T(128)}) while((s32[]{:T(128)}, f32[32,1024]{1,0:T(8,128)S(1)}, f32[32,1024]{1,0:T(8,128)S(1)}, ...), condition=%wide.region_4.4_spmd.clone.clone, body=%wide.region_3.3_spmd.sunk.clone.clone.sunk | while | flops 499715 | bytes 3100039 | solution.py:68
  167.6 2.5 convert_element_type.73
  170.2 2.8 reshape.111
  172.9 146.6 %all_to_all.20 = bf16[16,2,32768]{2,1,0:T(2,128)(2,1)S(1)} all-to-all(bf16[16,2,32768]{2,1,0:T(2,128)(2,1)} %reshape.111), channel_id=1, replica_groups=mesh['row_0'=4,'row_1'=2,'col_0'=4,'col_1'=4] {'col_0','col_1'}, dimensions={0} | all-to-all | bytes 4194304 | tf_op jit(solution)/shard_map/all_to_all | solution.py:153
  322.2 3.5 copy.32
  325.7 3.7 all-to-all-start.2
  329.4 25.2 %all-to-all-done.2 = bf16[16,2,32768]{2,1,0:T(2,128)(2,1)S(1)} async-done(((bf16[16,2,32768]{2,1,0:T(2,128)(2,1)}), bf16[16,2,32768]{2,1,0:T(2,128)(2,1)S(1)}, u32[]{:S(2)}, u32[]{:S(2)}) %all-to-all-start.2) | async-done | bytes 2097184 | tf_op jit(solution)/shard_map/all_to_all | solution.py:146
  354.6 2.8 reshape.114
  359.9 117.8 %while.93 = (s32[]{:T(128)}, f32[32,32,1024]{2,1,0:T(8,128)}, f32[]{:T(128)}, s32[]{:T(128)}, s32[4,2]{0,1:T(2,128)S(1)}, /*index=5*/s32[64]{0:T(128)S(1)}, bf16...) while((s32[]{:T(128)}, f32[32,32,1024]{2,1,0:T(8,128)}, ...), condition=%wide.region_11.12_spmd.clone, body=%wide.region_7.11_spmd.sunk.clone.sunk | while | flops 761891 | bytes 5591080 | solution.py:102
  379.6 36.9 %while.95 = (s32[]{:T(128)}, f32[32,1024]{1,0:T(8,128)S(1)}, f32[32,1024]{1,0:T(8,128)S(1)}, f32[32,1024]{1,0:T(8,128)S(1)}, s32[]{:T(128)}, /*index=5*/f32[12]{0:T(128)S(1)}, f32[12]{0:T(128)S(1)}, s32[]{:T(128)}) while((s32[]{:T(128)}, f32[32,1024]{1,0:T(8,128)S(1)}, f32[32,1024]{1,0:T(8,128)S(1)}, ...), condition=%wide.region_9.9_spmd.clone.clone, body=%wide.region_8.8_spmd.sunk.clone.clone.sunk | while | flops 499715 | bytes 3100039 | solution.py:68
  438.2 36.9 %while.95 = (s32[]{:T(128)}, f32[32,1024]{1,0:T(8,128)S(1)}, f32[32,1024]{1,0:T(8,128)S(1)}, f32[32,1024]{1,0:T(8,128)S(1)}, s32[]{:T(128)}, /*index=5*/f32[12]{0:T(128)S(1)}, f32[12]{0:T(128)S(1)}, s32[]{:T(128)}) while((s32[]{:T(128)}, f32[32,1024]{1,0:T(8,128)S(1)}, f32[32,1024]{1,0:T(8,128)S(1)}, ...), condition=%wide.region_9.9_spmd.clone.clone, body=%wide.region_8.8_spmd.sunk.clone.clone.sunk | while | flops 499715 | bytes 3100039 | solution.py:68
  477.7 2.5 convert_element_type.76
  480.3 2.8 reshape.115
  483.0 122.9 %all-to-all-start.3 = ((bf16[16,2,32768]{2,1,0:T(2,128)(2,1)}), bf16[16,2,32768]{2,1,0:T(2,128)(2,1)S(1)}, u32[]{:S(2)}, u32[]{:S(2)}) async-start(bf16[16,2,32768]{2,1,0:T(2,128)(2,1)} %reshape.115), calls=%async_computation.3 | async-start | bytes 4194304 | tf_op jit(solution)/shard_map/all_to_all | solution.py:153
  606.0 8.4 %psum.28 = f32[2]{0:T(128)S(1)} all-reduce(f32[2]{0:T(128)S(1)} %pad_maximum_fusion), channel_id=1, replica_groups=mesh['row_0'=4,'row_1'=2,'col_0'=4,'col_1'=4] {'row_0'}, use_global_device_ids=true, to_apply=%region_12.13 | all-reduce | flops 2 | bytes 16 | tf_op jit(solution)/shard_map/psum | solution.py:22
  614.4 8.1 %psum.29 = f32[2]{0:T(128)S(1)} all-reduce(f32[2]{0:T(128)S(1)} %psum.28), channel_id=1, replica_groups=mesh['row_0'=4,'row_1'=2,'col_0'=4,'col_1'=4] {'row_1'}, use_global_device_ids=true, to_apply=%region_13.14 | all-reduce | flops 2 | bytes 16 | tf_op jit(solution)/shard_map/psum | solution.py:22
  622.5 10.5 %psum.30 = f32[2]{0:T(128)S(1)} all-reduce(f32[2]{0:T(128)S(1)} %psum.29), channel_id=1, replica_groups=mesh['row_0'=4,'row_1'=2,'col_0'=4,'col_1'=4] {'col_0'}, use_global_device_ids=true, to_apply=%region_14.15 | all-reduce | flops 2 | bytes 16 | tf_op jit(solution)/shard_map/psum | solution.py:22
  633.0 8.2 %psum.31 = f32[2]{0:T(128)S(1)} all-reduce(f32[2]{0:T(128)S(1)} %psum.30), channel_id=1, replica_groups=mesh['row_0'=4,'row_1'=2,'col_0'=4,'col_1'=4] {'col_1'}, use_global_device_ids=true, to_apply=%region_15.16 | all-reduce | flops 2 | bytes 16 | tf_op jit(solution)/shard_map/psum | solution.py:22
  (441 shorter events, 188.4 us)
Async XLA Ops:
  0.6 17.5 %copy-start = (s32[512,3]{0,1:T(4,128)S(1)}, s32[512,3]{0,1:T(4,128)}, u32[]{:S(2)}) copy-start(s32[512,3]{0,1:T(4,128)} %param.17) | copy-start | bytes 18436
  7.9 8.7 %copy-start.4 = (s32[16]{0:T(128)S(1)}, s32[16]{0:T(128)}, u32[]{:S(2)}) copy-start(s32[16]{0:T(128)} %param.19) | copy-start | bytes 196
  7.9 36.6 %all-to-all-start = ((bf16[16,2,32768]{2,1,0:T(2,128)(2,1)}), bf16[16,2,32768]{2,1,0:T(2,128)(2,1)S(1)}, u32[]{:S(2)}, u32[]{:S(2)}) async-start(bf16[16,2,32768]{2,1,0:T(2,128)(2,1)} %copy.30), calls=%async_computation | async-start | bytes 4194304 | tf_op jit(solution)/shard_map/all_to_all | solution.py:146
  47.3 2.5 copy-start.5
  47.3 2.5 copy-start.6
  319.5 1.3 copy-start.1
  319.5 1.3 copy-start.2
  325.7 28.9 %all-to-all-start.2 = ((bf16[16,2,32768]{2,1,0:T(2,128)(2,1)}), bf16[16,2,32768]{2,1,0:T(2,128)(2,1)S(1)}, u32[]{:S(2)}, u32[]{:S(2)}) async-start(bf16[16,2,32768]{2,1,0:T(2,128)(2,1)} %copy.32), calls=%async_computation.2 | async-start | bytes 4194304 | tf_op jit(solution)/shard_map/all_to_all | solution.py:146
  483.0 158.7 %all-to-all-start.3 = ((bf16[16,2,32768]{2,1,0:T(2,128)(2,1)}), bf16[16,2,32768]{2,1,0:T(2,128)(2,1)S(1)}, u32[]{:S(2)}, u32[]{:S(2)}) async-start(bf16[16,2,32768]{2,1,0:T(2,128)(2,1)} %reshape.115), calls=%async_computation.3 | async-start | bytes 4194304 | tf_op jit(solution)/shard_map/all_to_all | solution.py:153
  641.7 1.3 copy-start.3
where the time goes:
time: 654 us; the launch traced here: 644 us
  blocking collectives  182 us (28%)
  starting transfers between devices  135 us (21%)
  local copies, waits for them, and re-layouts  114 us (17%)
  other arithmetic  93 us (14%)
  loops' own time  63.5 us (10%)
  waiting for transfers between devices  51.5 us (8%)
    all_to_all x1, blocking collectives, local(): lax.all_to_all(slot_terms, COL, split_axis=0, concat_axis=0, tiled=True)  147 us
    all_to_all x1, starting transfers between devices, local(): lax.all_to_all(slot_terms, COL, split_axis=0, concat_axis=0, tiled=True)  123 us
    add x48, other arithmetic, sweep(): direction = keep_coef[index] * direction + mix_coef[index] * remainder  72.3 us
    dynamic_slice x96, local copies, waits for them, and re-layouts, sweep(): direction = keep_coef[index] * direction + mix_coef[index] * remainder  63.1 us
    another operation x2, loops' own time, run_pairs(): lax.fori_loop(0, mine_count, one_pair, (collected, jnp.zeros((), jnp.floa...  61.2 us
    all_to_all x2, waiting for transfers between devices, local(): lax.all_to_all(outgoing, COL, split_axis=0, concat_axis=0, tiled=True)  51.5 us
    psum x4, blocking collectives, by_axis(): x = lax.psum(x, axis)  35.2 us
  transfers between devices with their start and end apart: 3, of which 2 were waited for; matrix products, arithmetic and copies ran while one was open for 0% of the time, Pallas kernels for 0%

commit v1 on v0

v1 whole, which is shorter than its diff:
```python
import functools

import jax
import jax.numpy as jnp
import ml_dtypes
import numpy as np
from jax import lax
from jax.experimental import pallas as pl
from jax.experimental.pallas import tpu as pltpu
from jax.sharding import PartitionSpec as P

SWEEPS = 12
ROUNDS = 2
TILE_R = 16
TILE_C = 128
screen_mu = 0.1
damping = 0.5


def spectral_tables(edge):
    k = np.arange(1, edge + 1)
    basis = np.sqrt(2.0 / (edge + 1)) * np.sin(np.pi * np.outer(k, k) / (edge + 1))
    line = 2.0 * np.cos(np.pi * k / (edge + 1))
    eig = (6.0 + screen_mu) - (line[:, None, None] + line[None, :, None] + line[None, None, :])
    c, h = 6.0 + screen_mu, 6.0
    g = c / h
    q = 1.0 / g
    u = np.zeros_like(eig)
    t = np.ones_like(eig)
    d = t / c
    for _ in range(SWEEPS):
        u = u + d
        t = t - eig * d
        q_new = 1.0 / (2.0 * g - q)
        d = q_new * q * d + (2.0 * q_new / h) * t
        q = q_new
    return basis, u.reshape(edge, edge * edge)


def two_parts(x):
    high = x.astype(ml_dtypes.bfloat16)
    return np.stack([high, (x - high.astype(np.float64)).astype(ml_dtypes.bfloat16)])


def split(x):
    high = x.astype(jnp.bfloat16)
    return high, (x - high.astype(jnp.float32)).astype(jnp.bfloat16)


def dot(a, b):
    return jnp.dot(a, b, preferred_element_type=jnp.float32)


def dot_split(a, b):
    (a_high, a_low), (b_high, b_low) = a, b
    return dot(a_high, b_high) + (dot(a_low, b_high) + dot(a_high, b_low))


def peers(n_col):
    side = int(round(n_col**0.5))
    steps = [(a, b) for a in range(side) for b in range(side) if a + b > 0]
    return side, sorted(steps, key=lambda p: -(min(p[0], side - p[0]) + min(p[1], side - p[1])))


def kernel(
    n_row,
    n_col,
    S,
    tbl,
    orb_hbm,
    grad_hbm,
    kron_hbm,
    sx_hbm,
    poly_hbm,
    exb,
    energy_out,
    orb,
    grad,
    kron,
    sx,
    poly,
    box_stage,
    q_stage,
    slab0,
    q_slab,
    slab1,
    pack,
    pair_box,
    partner,
    density,
    term_stage,
    terms,
    wide,
    summed,
    final_stage,
    e_mine,
    e_group,
    e_sum,
    e_row,
    first_of,
    second_of,
    load_sem,
    send_sem,
    recv_sem,
):
    me = lax.axis_index("col")
    row = lax.axis_index("row")
    own, edge, plane = orb.shape
    norb = own * n_col
    slots = S * n_col
    halves = edge // TILE_R
    strips = plane // TILE_C

    loads = [
        pltpu.make_async_copy(a, b, load_sem.at[i])
        for i, (a, b) in enumerate(
            ((orb_hbm, orb), (grad_hbm, grad), (kron_hbm, kron), (sx_hbm, sx), (poly_hbm, poly))
        )
    ]
    for one in loads:
        one.start()

    barrier = pltpu.get_barrier_semaphore()

    def greet_col(d, _):
        pl.semaphore_signal(barrier, inc=1, device_id={"col": (me + d) % n_col}, device_id_type=pl.DeviceIdType.MESH)
        return 0

    def greet_row(d, _):
        pl.semaphore_signal(barrier, inc=1, device_id={"row": (row + d) % n_row}, device_id_type=pl.DeviceIdType.MESH)
        return 0

    lax.fori_loop(1, n_col, greet_col, 0)
    lax.fori_loop(1, n_row, greet_row, 0)

    count_at = n_col * 8
    offset_at = count_at + n_col

    def rank(r, firsts):
        def seek(p, state):
            start, found = state
            count = tbl[count_at + p]
            inside = (r >= start) & (r < start + count)
            return start + count, jnp.where(inside, p * 4 + r - start, found)

        total, found = lax.fori_loop(0, n_col, seek, (jnp.int32(0), jnp.int32(-1)))
        at = jnp.maximum(found, 0) * 2
        first = tbl[at]
        first_of[r] = first
        second_of[r] = tbl[at + 1]
        lane = lax.broadcasted_iota(jnp.int32, (norb, slots), 1)
        return jnp.where(lane == r, jnp.where(found >= 0, first, -1), firsts)

    firsts = lax.fori_loop(0, slots, rank, jnp.full((norb, slots), -1, jnp.int32))
    choose = (lax.broadcasted_iota(jnp.int32, (norb, slots), 0) == firsts).astype(jnp.float32).astype(jnp.bfloat16)

    def total_live(p, acc):
        return acc + tbl[count_at + p]

    live_total = lax.fori_loop(0, n_col, total_live, jnp.int32(0))

    def tile_of(s):
        return pl.ds(pl.multiple_of((s // strips) * TILE_R, TILE_R), TILE_R), pl.ds(
            pl.multiple_of((s % strips) * TILE_C, TILE_C), TILE_C
        )

    my_rows, my_cols = tile_of(me)

    def exchange(src_of, dst, which, before=None):
        side, steps = peers(n_col)
        for dy, dz in steps:
            to = ((me // side + dy) % side) * side + (me % side + dz) % side
            if before is not None:
                before(to)
            pltpu.make_async_remote_copy(
                src_ref=src_of(to),
                dst_ref=dst,
                send_sem=send_sem.at[which],
                recv_sem=recv_sem.at[which],
                device_id={"col": to},
                device_id_type=pl.DeviceIdType.MESH,
            ).start()
        if before is not None:
            before(me)
        pltpu.make_async_copy(src_of(me), dst, recv_sem.at[which]).start()

    def arrived(ref, which):
        pltpu.make_async_copy(ref, ref, recv_sem.at[which]).wait()

    def sent(ref, which):
        pltpu.make_async_copy(ref, ref, send_sem.at[which]).wait()

    loads[0].wait()
    box_stage[...] = orb[...].astype(jnp.bfloat16)
    pl.semaphore_wait(barrier, n_col - 1 + n_row - 1)

    def from_boxes(s):
        rows, cols = tile_of(s)
        return box_stage.at[:, rows, cols]

    def from_q(s):
        rows, cols = tile_of(s)
        return q_stage.at[:, rows, cols]

    mine4 = pl.ds(me * own, own)
    exchange(from_boxes, slab0.at[mine4], 0)
    loads[1].wait()
    q_stage[...] = orb[...] - damping * grad[...]
    exchange(from_q, q_slab.at[mine4], 1)
    for one in loads[2:]:
        one.wait()

    energies = []
    for r in range(ROUNDS):
        slab = (slab0, slab1)[r]
        if r == 0:
            arrived(slab0, 0)

        def fill(p):
            for k in range(S):
                pack[r, p * 2 * S + 2 * k] = slab[first_of[p * S + k]]
                pack[r, p * 2 * S + 2 * k + 1] = slab[second_of[p * S + k]]

        def from_pack(p):
            return pack.at[r, pl.ds(p * 2 * S, 2 * S)]

        exchange(from_pack, pair_box.at[r, :, my_rows, my_cols], 2 + 2 * r, fill)
        arrived(pair_box.at[r], 2 + 2 * r)

        lane = lax.broadcasted_iota(jnp.int32, (edge, plane), 1)
        line = lax.broadcasted_iota(jnp.int32, (edge, plane), 0)
        for k in range(S):
            a = offset_at + 3 * first_of[me * S + k]
            b = offset_at + 3 * second_of[me * S + k]
            dx = tbl[a] - tbl[b]
            dy = tbl[a + 1] - tbl[b + 1]
            dz = tbl[a + 2] - tbl[b + 2]
            t = dy * edge + dz
            moved = pair_box[r, 2 * k + 1].astype(jnp.float32)
            moved = pltpu.roll(moved, lax.rem(plane - t, jnp.int32(plane)), 1)
            moved = pltpu.roll(moved, lax.rem(edge - dx, jnp.int32(edge)), 0)
            at_x = line + dx
            at_y = lane // edge + dy
            at_z = lane % edge + dz
            inside = (
                (at_x >= 0) & (at_x < edge) & (at_y >= 0) & (at_y < edge) & (at_z >= 0) & (at_z < edge)
            )
            moved = jnp.where(inside, moved, 0.0)
            partner[pl.ds(k * edge, edge), :] = moved
            density[pl.ds(k * edge, edge), :] = pair_box[r, 2 * k].astype(jnp.float32) * moved

        yz = kron[0], kron[1]
        along_x = sx[0], sx[1]
        modes = dot_split(split(density[...]), yz)
        modes = dot_split(along_x, split(modes)).reshape(S, edge, plane) * poly[...][None]
        modes = dot_split(along_x, split(modes.reshape(S * edge, plane)))
        potential = dot_split(split(modes), yz)
        term_stage[r] = (potential * partner[...]).astype(jnp.bfloat16).reshape(S, edge, plane)
        cells = (density[...] * potential).reshape(S, edge, plane)
        energy = jnp.zeros((edge, plane), jnp.float32)
        for k in range(S):
            energy = energy + jnp.where(me * S + k < live_total, cells[k], 0.0)
        energies.append(energy)

        def from_terms(s):
            rows, cols = tile_of(s)
            return term_stage.at[r, :, rows, cols]

        exchange(from_terms, terms.at[r, pl.ds(me * S, S)], 3 + 2 * r)

        if r == ROUNDS - 1:
            for i, e in enumerate(energies):
                part = jnp.sum(e.reshape(edge // 8, 8, plane), axis=0)
                e_mine[i] = sum(part[:, c * TILE_C : (c + 1) * TILE_C] for c in range(strips))
            exchange(lambda s: e_mine, e_group.at[me], 7)

        arrived(terms.at[r], 3 + 2 * r)
        wide[...] = terms[r].astype(jnp.float32).reshape(slots * TILE_R, TILE_C)
        if r == 0:
            arrived(q_slab, 1)
        for j in range(TILE_R):
            part = wide[pl.ds(j, slots, stride=TILE_R), :].astype(jnp.bfloat16)
            out = dot(choose, part)
            if r == 0:
                summed[pl.ds(j, norb, stride=TILE_R), :] = out
            else:
                summed[pl.ds(j, norb, stride=TILE_R), :] += out
        if r == 0:
            total = summed[...].reshape(norb, TILE_R, TILE_C)
            slab1[...] = (q_slab[...] - damping * total).astype(jnp.bfloat16)
        else:
            final_stage[...] = summed[...].reshape(norb, TILE_R, TILE_C).astype(jnp.bfloat16)

    exchange(lambda s: final_stage.at[pl.ds(s * own, own)], exb.at[:, my_rows, my_cols], 6)

    arrived(e_group, 7)
    e_sum[...] = jnp.sum(e_group[...], axis=0)

    def go_row(d, _):
        pltpu.make_async_remote_copy(
            src_ref=e_sum,
            dst_ref=e_row.at[row],
            send_sem=send_sem.at[8],
            recv_sem=recv_sem.at[8],
            device_id={"row": (row + d) % n_row},
            device_id_type=pl.DeviceIdType.MESH,
        ).start()
        return 0

    lax.fori_loop(1, n_row, go_row, 0)
    pltpu.make_async_copy(e_sum, e_row.at[row], recv_sem.at[8]).start()
    arrived(e_row, 8)
    all_cells = edge * edge * edge * n_row * n_col
    for i in range(ROUNDS):
        energy_out[i] = jnp.sum(jnp.sum(e_row[:, i], axis=0)) / all_cells
    arrived(exb, 6)

    others = n_col - 1
    sent(slab0.at[pl.ds(0, others * own)], 0)
    sent(q_slab.at[pl.ds(0, others * own)], 1)
    for r in range(ROUNDS):
        sent(pack.at[r, pl.ds(0, others * 2 * S)], 2 + 2 * r)
        sent(terms.at[r, pl.ds(0, others * S)], 3 + 2 * r)
    sent(final_stage.at[pl.ds(0, others * own)], 6)
    sent(e_group.at[pl.ds(0, others)], 7)
    if n_row > 1:
        sent(e_row.at[pl.ds(0, n_row - 1)], 8)


def local(n_row, n_col, S, orbitals, gradient, offsets, pairs, counts):
    own, edge, plane = orbitals.shape
    norb = own * n_col
    slots = S * n_col
    base = lax.axis_index("row") * norb
    table = jnp.concatenate(
        [
            (pairs - base).reshape(-1),
            counts,
            lax.dynamic_slice_in_dim(offsets, base, norb, 0).reshape(-1),
        ]
    )
    basis, poly = spectral_tables(edge)
    kron = two_parts(np.kron(basis, basis))
    sx = two_parts(np.kron(np.eye(S), basis))
    hbm = pl.BlockSpec(memory_space=pltpu.HBM)
    f32, bf16 = jnp.float32, jnp.bfloat16
    tiles = (norb, TILE_R, TILE_C)
    exchanged, energies = pl.pallas_call(
        functools.partial(kernel, n_row, n_col, S),
        out_shape=(
            jax.ShapeDtypeStruct((own, edge, plane), bf16),
            jax.ShapeDtypeStruct((ROUNDS,), f32),
        ),
        in_specs=[pl.BlockSpec(memory_space=pltpu.SMEM)] + [hbm] * 5,
        out_specs=(pl.BlockSpec(memory_space=pltpu.VMEM), pl.BlockSpec(memory_space=pltpu.SMEM)),
        scratch_shapes=[
            pltpu.VMEM((own, edge, plane), f32),
            pltpu.VMEM((own, edge, plane), f32),
            pltpu.VMEM((2, plane, plane), bf16),
            pltpu.VMEM((2, S * edge, S * edge), bf16),
            pltpu.VMEM((edge, plane), f32),
            pltpu.VMEM((own, edge, plane), bf16),
            pltpu.VMEM((own, edge, plane), f32),
            pltpu.VMEM(tiles, bf16),
            pltpu.VMEM(tiles, f32),
            pltpu.VMEM(tiles, bf16),
            pltpu.VMEM((ROUNDS, slots * 2, TILE_R, TILE_C), bf16),
            pltpu.VMEM((ROUNDS, 2 * S, edge, plane), bf16),
            pltpu.VMEM((S * edge, plane), f32),
            pltpu.VMEM((S * edge, plane), f32),
            pltpu.VMEM((ROUNDS, S, edge, plane), bf16),
            pltpu.VMEM((ROUNDS, slots, TILE_R, TILE_C), bf16),
            pltpu.VMEM((slots * TILE_R, TILE_C), f32),
            pltpu.VMEM((norb * TILE_R, TILE_C), f32),
            pltpu.VMEM(tiles, bf16),
            pltpu.VMEM((ROUNDS, 8, TILE_C), f32),
            pltpu.VMEM((n_col, ROUNDS, 8, TILE_C), f32),
            pltpu.VMEM((ROUNDS, 8, TILE_C), f32),
            pltpu.VMEM((n_row, ROUNDS, 8, TILE_C), f32),
            pltpu.SMEM((slots,), jnp.int32),
            pltpu.SMEM((slots,), jnp.int32),
            pltpu.SemaphoreType.DMA((5,)),
            pltpu.SemaphoreType.DMA((9,)),
            pltpu.SemaphoreType.DMA((9,)),
        ],
        compiler_params=pltpu.CompilerParams(
            collective_id=S, has_side_effects=True, vmem_limit_bytes=60 * 1024 * 1024
        ),
    )(table, orbitals, gradient, jnp.asarray(kron), jnp.asarray(sx), jnp.asarray(poly.astype(np.float32)))
    updated = orbitals - gradient - damping * exchanged.astype(f32)
    return updated, energies


def solution(mesh):
    n_row, n_col = mesh.shape["row"], mesh.shape["col"]
    both = P(("row", "col"), None, None)
    return jax.shard_map(
        functools.partial(local, n_row, n_col, 4),
        mesh=mesh,
        in_specs=(both, both, P(), P("row", None, None), P("row")),
        out_specs=(both, P()),
        check_vma=False,
    )
```

time: 654 us -> 70.4 us (0.11); the launches traced: 644 us -> 70.2 us
  blocking collectives: 182 us -> 0 us
  starting transfers between devices: 135 us -> 0 us
  local copies, waits for them, and re-layouts: 114 us -> 2.42 us
  other arithmetic: 93 us -> 3.85 us
  loops' own time: 63.5 us -> 0 us
  Pallas kernels: 0 us -> 63.2 us
  waiting for transfers between devices: 51.5 us -> 0 us
    all_to_all x1 -> x0, blocking collectives: 147 us -> none  [local(): lax.all_to_all(slot_terms, COL, split_axis=0, concat_axis=0, tiled=True)]
    all_to_all x3 -> x0, starting transfers between devices: 135 us -> none  [the longest x1 123 us: local(): lax.all_to_all(slot_terms, COL, split_axis=0, concat_axis=0, tiled=True)]
    dynamic_slice x117 -> x2, local copies, waits for them, and re-layouts: 76.8 us -> 0.17 us  [local(): lax.dynamic_slice_in_dim(offsets, base, norb, 0).reshape(-1)]
    add x53 -> x0, other arithmetic: 72.6 us -> none  [the longest x48 72.3 us: sweep(): direction = keep_coef[index] * direction + mix_coef[index] * remainder]
    another operation x6 -> x0, loops' own time: 63.5 us -> none  [the longest x2 61.2 us: run_pairs(): lax.fori_loop(0, mine_count, one_pair, (collected, jnp.zeros((), jnp.floa...]
    pallas_call x0 -> x1, Pallas kernels: none -> 63.2 us  [local(): pl.pallas_call(functools.partial(kernel, n_row, n_col, S), out_shape=(jax...]
    all_to_all x3 -> x0, waiting for transfers between devices: 51.5 us -> none  [the longest x2 51.5 us: local(): lax.all_to_all(outgoing, COL, split_axis=0, concat_axis=0, tiled=True)]
    psum x4 -> x0, blocking collectives: 35.2 us -> none  [by_axis(): x = lax.psum(x, axis)]
  transfers between devices with their start and end apart: 3 -> 0, of which waited for: 2 -> 0; matrix products, arithmetic and copies ran while one was open for 0% -> 0% of each run, Pallas kernels for 0% -> 0%
where the time goes in v1:
time: 70.4 us; the launch traced here: 70.2 us
  Pallas kernels  63.2 us (90%)
  other arithmetic  3.85 us (5%)
  local copies, waits for them, and re-layouts  2.42 us (3%)
    pallas_call x1, Pallas kernels, local(): pl.pallas_call(functools.partial(kernel, n_row, n_col, S), out_shape=(jax...  63.2 us
    unnamed x7, local copies, waits for them, and re-layouts  1.86 us
    sub x1, other arithmetic, local(): updated = orbitals - gradient - damping * exchanged.astype(f32)  1.85 us

profile of v1, /device:TPU:1, one launch (start us, length us, event | category | flops | bytes accessed | tf_op | source)
XLA Modules:
  0.0 70.2 jit_solution(14818453082841791279)
XLA Ops:
  0.6 0.0 copy-start
  0.6 0.0 copy-start.2
  0.7 0.0 copy-start.1
  0.7 0.7 copy-done
  1.3 0.1 constant_dynamic-slice_fusion
  1.4 0.7 broadcast_subtract_fusion
  2.1 0.1 copy.11
  2.2 0.1 reshape.10
  2.4 0.1 copy.12
  2.5 0.1 reshape.11
  2.6 1.3 %pad_add_fusion.tbl = s32[336]{0:T(512)} fusion(s32[192]{0:T(256)S(1)} %reshape.11, s32[16]{0:T(128)} %param.12, s32[128]{0:T(128)S(1)} %reshape.10), kind=kLoop, calls=%fused_computation.1 | loop fusion | flops 672 | bytes 2688 | tf_op jit(solution)/shard_map/concatenate | solution.py:335
  3.9 63.2 %shard_map.95 = (bf16[4,32,1024]{2,1,0:T(8,128)(2,1)}, f32[2]{0:T(128)}) custom-call(s32[336]{0:T(512)} %pad_add_fusion.tbl, f32[4,32,1024]{2,1,0:T(8,128)} %orb_hbm.1, f32[4,32,1024]{2,1,0:T(8,128)} %grad_hbm.1, bf16[2,1024,1024]{2,1,0:T(8,128)(2,1)} %constant.20.clone.kron_hbm, bf16[2,128,128]{2,1,0:T(8,128)(2,1)} %constant.21.clone.sx_hbm, ...), custom_call_target="tpu_custom_call" | custom-call | tf_op jit(solution)/shard_map/pallas_call | solution.py:348
  67.1 0.0 copy-done.2
  67.1 0.0 copy-done.1
  67.1 1.9 %multiply_subtract_fusion = f32[4,32,1024]{2,1,0:T(8,128)} fusion(bf16[4,32,1024]{2,1,0:T(8,128)(2,1)} %get-tuple-element.4, f32[4,32,1024]{2,1,0:T(8,128)S(1)} %copy-done.1, f32[4,32,1024]{2,1,0:T(8,128)S(1)} %copy-done.2), kind=kLoop, calls=%fused_computation | loop fusion | flops 524288 | bytes 1835008 | tf_op jit(solution)/shard_map/sub | solution.py:390
  69.0 1.2 %copy.14 = f32[2]{0:T(128)} copy(f32[2]{0:T(128)} %get-tuple-element.9) | data formatting | bytes 16
Async XLA Ops:
  0.6 0.7 %copy-start = (s32[512,3]{0,1:T(4,128)S(1)}, s32[512,3]{0,1:T(4,128)}, u32[]{:S(2)}) copy-start(s32[512,3]{0,1:T(4,128)} %param.10) | copy-start | bytes 18436
  0.6 66.5 %copy-start.2 = (f32[4,32,1024]{2,1,0:T(8,128)S(1)}, f32[4,32,1024]{2,1,0:T(8,128)}, u32[]{:S(2)}) copy-start(f32[4,32,1024]{2,1,0:T(8,128)} %grad_hbm.1) | copy-start | bytes 1572868
  0.7 66.5 %copy-start.1 = (f32[4,32,1024]{2,1,0:T(8,128)S(1)}, f32[4,32,1024]{2,1,0:T(8,128)}, u32[]{:S(2)}) copy-start(f32[4,32,1024]{2,1,0:T(8,128)} %orb_hbm.1) | copy-start | bytes 1572868

commit v2 on v1

--- a/solution.py
+++ b/solution.py
@@ -62,7 +62,7 @@
     return side, sorted(steps, key=lambda p: -(min(p[0], side - p[0]) + min(p[1], side - p[1])))
 
 
-def kernel(
+def spread_kernel(
     n_row,
     n_col,
     S,
@@ -327,7 +327,7 @@
         sent(e_row.at[pl.ds(0, n_row - 1)], 8)
 
 
-def local(n_row, n_col, S, orbitals, gradient, offsets, pairs, counts):
+def spread_pairs(n_row, n_col, S, orbitals, gradient, offsets, pairs, counts):
     own, edge, plane = orbitals.shape
     norb = own * n_col
     slots = S * n_col
@@ -346,7 +346,7 @@
     f32, bf16 = jnp.float32, jnp.bfloat16
     tiles = (norb, TILE_R, TILE_C)
     exchanged, energies = pl.pallas_call(
-        functools.partial(kernel, n_row, n_col, S),
+        functools.partial(spread_kernel, n_row, n_col, S),
         out_shape=(
             jax.ShapeDtypeStruct((own, edge, plane), bf16),
             jax.ShapeDtypeStruct((ROUNDS,), f32),
@@ -391,11 +391,360 @@
     return updated, energies
 
 
+def direct_kernel(
+    n_row,
+    n_col,
+    REMOTE,
+    LOCAL,
+    pairs,
+    counts,
+    offsets,
+    orb_hbm,
+    grad_hbm,
+    kron_hbm,
+    sx_hbm,
+    poly_hbm,
+    exchanged,
+    energy_out,
+    orb,
+    grad,
+    kron,
+    sx,
+    poly,
+    stage0,
+    stage1,
+    slab0,
+    slab1,
+    pack,
+    pair_box,
+    partner,
+    density,
+    e_mine,
+    e_group,
+    e_sum,
+    e_row,
+    slot_rows,
+    slot_of,
+    load_sem,
+    slot_sem,
+    send_sem,
+    recv_sem,
+):
+    me = lax.axis_index("col")
+    row = lax.axis_index("row")
+    own, edge, plane = orb.shape
+    norb = own * n_col
+    base = row * norb
+    strips = plane // TILE_C
+    per_owner = pairs.shape[0]
+    mesh_id = pl.DeviceIdType.MESH
+    box_stage, slab = (stage0, stage1), (slab0, slab1)
+
+    loads = [
+        pltpu.make_async_copy(a, b, load_sem.at[i])
+        for i, (a, b) in enumerate(
+            ((orb_hbm, orb), (grad_hbm, grad), (kron_hbm, kron), (sx_hbm, sx), (poly_hbm, poly))
+        )
+    ]
+    for one in loads:
+        one.start()
+
+    barrier = pltpu.get_barrier_semaphore()
+    side, steps = peers(n_col)
+
+    def peer(step):
+        return ((me // side + step[0]) % side) * side + (me % side + step[1]) % side
+
+    for step in steps:
+        pl.semaphore_signal(barrier, inc=1, device_id={"col": peer(step)}, device_id_type=mesh_id)
+
+    def greet_row(d, _):
+        pl.semaphore_signal(barrier, inc=1, device_id={"row": (row + d) % n_row}, device_id_type=mesh_id)
+        return 0
+
+    lax.fori_loop(1, n_row, greet_row, 0)
+
+    lane = lax.broadcasted_iota(jnp.int32, (8, TILE_C), 1)
+
+    def place(index, state):
+        p, k = index // per_owner, index % per_owner
+        at_first = lax.div(pairs[k, 0, p] - base, jnp.int32(own))
+        at_second = lax.div(pairs[k, 1, p] - base, jnp.int32(own))
+        here = jnp.where(k < counts[p], at_first, -1)
+        far = jnp.where(at_first == at_second, -1, here)
+        near = jnp.where(at_first == at_second, here, -1)
+        out = []
+        for device, (count, slots) in zip((far, near), state):
+            hit = lane == device
+            slots = tuple(jnp.where(hit & (count == s), index, held) for s, held in enumerate(slots))
+            out.append((count + hit.astype(jnp.int32), slots))
+        return tuple(out)
+
+    none = jnp.full((8, TILE_C), -1, jnp.int32)
+    zero = jnp.zeros((8, TILE_C), jnp.int32)
+    (far_count, far_slots), (near_count, near_slots) = lax.fori_loop(
+        0, n_col * per_owner, place, ((zero, (none,) * REMOTE), (zero, (none,) * LOCAL))
+    )
+    for s, held in enumerate(far_slots + near_slots):
+        slot_rows[pl.ds(s, 1), :] = held[0:1, :]
+    over = ((far_count > REMOTE) | (near_count > LOCAL)).astype(jnp.float32)
+    overflow = jnp.sum(over[0:1, :], axis=1, keepdims=True)
+    to_scalars = pltpu.make_async_copy(slot_rows, slot_of, slot_sem.at[0])
+    to_scalars.start()
+
+    def tile_of(s):
+        return pl.ds(pl.multiple_of((s // strips) * TILE_R, TILE_R), TILE_R), pl.ds(
+            pl.multiple_of((s % strips) * TILE_C, TILE_C), TILE_C
+        )
+
+    my_rows, my_cols = tile_of(me)
+
+    def send(src, dst, which, to):
+        pltpu.make_async_remote_copy(
+            src_ref=src,
+            dst_ref=dst,
+            send_sem=send_sem.at[which],
+            recv_sem=recv_sem.at[which],
+            device_id={"col": to},
+            device_id_type=mesh_id,
+        ).start()
+
+    def arrived(ref, which):
+        pltpu.make_async_copy(ref, ref, recv_sem.at[which]).wait()
+
+    def sent(ref, which):
+        pltpu.make_async_copy(ref, ref, send_sem.at[which]).wait()
+
+    def send_boxes(r):
+        def part(s):
+            rows, cols = tile_of(s)
+            return box_stage[r].at[:, rows, cols]
+
+        dst = slab[r].at[pl.ds(me * own, own)]
+        for step in steps:
+            send(part(peer(step)), dst, 2 * r, peer(step))
+        pltpu.make_async_copy(part(me), dst, recv_sem.at[2 * r]).start()
+
+    def send_pairs(r):
+        dst = pair_box.at[r, :, my_rows, my_cols]
+
+        def fill(to):
+            for s in range(REMOTE):
+                index = jnp.maximum(slot_of[s, to], 0)
+                second = pairs[lax.rem(index, jnp.int32(per_owner)), 1, lax.div(index, jnp.int32(per_owner))]
+                pack[r, to, s] = slab[r][jnp.clip(second - base, 0, norb - 1)]
+
+        for step in steps:
+            fill(peer(step))
+            send(pack.at[r, peer(step)], dst, 2 * r + 1, peer(step))
+        fill(me)
+        pltpu.make_async_copy(pack.at[r, me], dst, recv_sem.at[2 * r + 1]).start()
+
+    line = lax.broadcasted_iota(jnp.int32, (edge, plane), 0)
+    cell = lax.broadcasted_iota(jnp.int32, (edge, plane), 1)
+
+    def work(r, start, number, between=None):
+        firsts = []
+        for n in range(number):
+            code = slot_of[start + n, me]
+            index = jnp.maximum(code, 0)
+            p = lax.div(index, jnp.int32(per_owner))
+            k = lax.rem(index, jnp.int32(per_owner))
+            first, second = pairs[k, 0, p], pairs[k, 1, p]
+            mine = jnp.clip(first - base - me * own, 0, own - 1)
+            firsts.append(jnp.where(code >= 0, mine, -1))
+            dx = offsets[0, first] - offsets[0, second]
+            dy = offsets[1, first] - offsets[1, second]
+            dz = offsets[2, first] - offsets[2, second]
+            t = dy * edge + dz
+            if start < REMOTE:
+                moved = pair_box[r, start + n]
+            else:
+                moved = box_stage[r][jnp.clip(second - base - me * own, 0, own - 1)]
+            moved = moved.astype(jnp.float32)
+            moved = pltpu.roll(moved, lax.rem(plane - t, jnp.int32(plane)), 1)
+            moved = pltpu.roll(moved, lax.rem(edge - dx, jnp.int32(edge)), 0)
+            at_x = line + dx
+            at_y = cell // edge + dy
+            at_z = cell % edge + dz
+            inside = (at_x >= 0) & (at_x < edge) & (at_y >= 0) & (at_y < edge) & (at_z >= 0) & (at_z < edge)
+            moved = jnp.where(inside, moved, 0.0)
+            partner[pl.ds(n * edge, edge), :] = moved
+            density[pl.ds(n * edge, edge), :] = box_stage[r][mine].astype(jnp.float32) * moved
+        rows = number * edge
+
+        def along_yz(x):
+            high, low = split(x)
+            both = dot(jnp.concatenate([high, low], 0), kron[0])
+            return both[:rows] + (both[rows:] + dot(high, kron[1]))
+
+        def along_x(x):
+            high, low = split(x)
+            part = sx[0, pl.ds(0, rows), pl.ds(0, rows)]
+            both = dot(jnp.concatenate([part, sx[1, pl.ds(0, rows), pl.ds(0, rows)]], 0), high)
+            return both[:rows] + (both[rows:] + dot(part, low))
+
+        modes = along_x(along_yz(density[pl.ds(0, rows), :])).reshape(number, edge, plane)
+        scaled = modes * poly[...][None]
+        energy = jnp.zeros((8, TILE_C), jnp.float32)
+        for n in range(number):
+            part = jnp.sum((modes[n] * scaled[n]).reshape(edge // 8, 8, plane), axis=0)
+            part = sum(part[:, c * TILE_C : (c + 1) * TILE_C] for c in range(strips))
+            energy = energy + jnp.where(firsts[n] >= 0, part, 0.0)
+        if between is not None:
+            between(energy)
+        potential = along_yz(along_x(scaled.reshape(rows, plane)))
+        terms = (potential * partner[pl.ds(0, rows), :]).astype(jnp.bfloat16).astype(jnp.float32)
+        for o in range(own):
+            total = exchanged[o]
+            for n in range(number):
+                total = total + jnp.where(firsts[n] == o, terms[n * edge : (n + 1) * edge], 0.0)
+            exchanged[o] = total
+        return energy
+
+    exchanged[...] = jnp.zeros_like(exchanged)
+    loads[0].wait()
+    box_stage[0][...] = orb[...].astype(jnp.bfloat16)
+    pl.semaphore_wait(barrier, n_col - 1 + n_row - 1)
+    send_boxes(0)
+    to_scalars.wait()
+    for one in loads[1:]:
+        one.wait()
+
+    def total_of(energy):
+        return jnp.sum(jnp.sum(energy, axis=0, keepdims=True), axis=1, keepdims=True)
+
+    half = LOCAL // 2
+    kept = []
+    for r in range(ROUNDS):
+        energy = work(r, REMOTE, half)
+        arrived(slab[r], 2 * r)
+        send_pairs(r)
+        energy = energy + work(r, REMOTE + half, LOCAL - half)
+        arrived(pair_box.at[r], 2 * r + 1)
+        if r < ROUNDS - 1:
+            kept.append(total_of(energy + work(r, 0, REMOTE)))
+            box_stage[r + 1][...] = (orb[...] - damping * ((r + 1.0) * grad[...] + exchanged[...])).astype(jnp.bfloat16)
+            send_boxes(r + 1)
+        else:
+
+            def send_energy(last):
+                values = kept + [total_of(energy + last), overflow]
+                at = lax.broadcasted_iota(jnp.int32, (1, TILE_C), 1)
+                out = jnp.zeros((1, TILE_C), jnp.float32)
+                for i, value in enumerate(values):
+                    out = jnp.where(at == i, value, out)
+                e_mine[...] = out
+                for step in steps:
+                    send(e_mine, e_group.at[me], 2 * ROUNDS, peer(step))
+                pltpu.make_async_copy(e_mine, e_group.at[me], recv_sem.at[2 * ROUNDS]).start()
+
+            work(r, 0, REMOTE, send_energy)
+
+    arrived(e_group, 2 * ROUNDS)
+    e_sum[...] = jnp.sum(e_group[...], axis=0)
+    last = 2 * ROUNDS + 1
+
+    def go_row(d, _):
+        pltpu.make_async_remote_copy(
+            src_ref=e_sum,
+            dst_ref=e_row.at[row],
+            send_sem=send_sem.at[last],
+            recv_sem=recv_sem.at[last],
+            device_id={"row": (row + d) % n_row},
+            device_id_type=mesh_id,
+        ).start()
+        return 0
+
+    lax.fori_loop(1, n_row, go_row, 0)
+    pltpu.make_async_copy(e_sum, e_row.at[row], recv_sem.at[last]).start()
+    others = n_col - 1
+    for r in range(ROUNDS):
+        sent(slab[r].at[pl.ds(0, others * own)], 2 * r)
+        sent(pack.at[r, pl.ds(0, others)], 2 * r + 1)
+    sent(e_group.at[pl.ds(0, others)], 2 * ROUNDS)
+    arrived(e_row, last)
+    energy_out[...] = jnp.sum(e_row[...], axis=0) / (edge * edge * edge * n_row * n_col)
+    if n_row > 1:
+        sent(e_row.at[pl.ds(0, n_row - 1)], last)
+
+
+def direct_pairs(n_row, n_col, REMOTE, LOCAL, orbitals, gradient, offsets, pairs, counts):
+    own, edge, plane = orbitals.shape
+    norb = own * n_col
+    basis, poly = spectral_tables(edge)
+    kron = two_parts(np.kron(basis, basis))
+    most = max(REMOTE, LOCAL - LOCAL // 2)
+    sx = two_parts(np.kron(np.eye(most), basis))
+    hbm = pl.BlockSpec(memory_space=pltpu.HBM)
+    smem = pl.BlockSpec(memory_space=pltpu.SMEM)
+    vmem = pl.BlockSpec(memory_space=pltpu.VMEM)
+    f32, bf16 = jnp.float32, jnp.bfloat16
+    return pl.pallas_call(
+        functools.partial(direct_kernel, n_row, n_col, REMOTE, LOCAL),
+        out_shape=(
+            jax.ShapeDtypeStruct((own, edge, plane), f32),
+            jax.ShapeDtypeStruct((1, TILE_C), f32),
+        ),
+        in_specs=[smem] * 3 + [hbm] * 5,
+        out_specs=(vmem, vmem),
+        scratch_shapes=[
+            pltpu.VMEM((own, edge, plane), f32),
+            pltpu.VMEM((own, edge, plane), f32),
+            pltpu.VMEM((2, plane, plane), bf16),
+            pltpu.VMEM((2, most * edge, most * edge), bf16),
+            pltpu.VMEM((edge, plane), f32),
+            pltpu.VMEM((own, edge, plane), bf16),
+            pltpu.VMEM((own, edge, plane), bf16),
+            pltpu.VMEM((norb, TILE_R, TILE_C), bf16),
+            pltpu.VMEM((norb, TILE_R, TILE_C), bf16),
+            pltpu.VMEM((ROUNDS, n_col, REMOTE, TILE_R, TILE_C), bf16),
+            pltpu.VMEM((ROUNDS, REMOTE, edge, plane), bf16),
+            pltpu.VMEM((most * edge, plane), f32),
+            pltpu.VMEM((most * edge, plane), f32),
+            pltpu.VMEM((1, TILE_C), f32),
+            pltpu.VMEM((n_col, 1, TILE_C), f32),
+            pltpu.VMEM((1, TILE_C), f32),
+            pltpu.VMEM((n_row, 1, TILE_C), f32),
+            pltpu.VMEM((16, TILE_C), jnp.int32),
+            pltpu.SMEM((16, TILE_C), jnp.int32),
+            pltpu.SemaphoreType.DMA((5,)),
+            pltpu.SemaphoreType.DMA((1,)),
+            pltpu.SemaphoreType.DMA((2 * ROUNDS + 2,)),
+            pltpu.SemaphoreType.DMA((2 * ROUNDS + 2,)),
+        ],
+        compiler_params=pltpu.CompilerParams(
+            collective_id=1, has_side_effects=True, vmem_limit_bytes=60 * 1024 * 1024
+        ),
+    )(
+        pairs.transpose(1, 2, 0),
+        counts,
+        offsets.T,
+        orbitals,
+        gradient,
+        jnp.asarray(kron),
+        jnp.asarray(sx),
+        jnp.asarray(poly.astype(np.float32)),
+    )
+
+
+def local(n_row, n_col, REMOTE, LOCAL, S, orbitals, gradient, offsets, pairs, counts):
+    exchanged, values = direct_pairs(n_row, n_col, REMOTE, LOCAL, orbitals, gradient, offsets, pairs, counts)
+
+    def enough():
+        return orbitals - gradient - damping * exchanged, values[0, :ROUNDS]
+
+    def general():
+        return spread_pairs(n_row, n_col, S, orbitals, gradient, offsets, pairs, counts)
+
+    return lax.cond(values[0, ROUNDS] > 0, general, enough)
+
+
 def solution(mesh):
     n_row, n_col = mesh.shape["row"], mesh.shape["col"]
     both = P(("row", "col"), None, None)
     return jax.shard_map(
-        functools.partial(local, n_row, n_col, 4),
+        functools.partial(local, n_row, n_col, 5, 6, 4),
         mesh=mesh,
         in_specs=(both, both, P(), P("row", None, None), P("row")),
         out_specs=(both, P()),

time: 70.4 us -> 48.9 us (0.69)
  Pallas kernels: 63.2 us -> 45.3 us
  other arithmetic: 3.85 us -> 0.89 us
  local copies, waits for them, and re-layouts: 2.42 us -> 1.13 us
  between operations: 0.69 us -> 1.41 us
    pallas_call x1, Pallas kernels: 63.2 us -> 45.3 us  [direct_pairs(): pl.pallas_call(functools.partial(direct_kernel, n_row, n_col, REMOTE, LOC...]
    sub x2 -> x1, other arithmetic: 2.54 us -> 0.89 us  [enough(): return (orbitals - gradient - damping * exchanged, values[0, :ROUNDS])]
    unnamed x7 -> x15, local copies, waits for them, and re-layouts: 1.86 us -> 0.55 us
    concatenate x1 -> x0, other arithmetic: 1.31 us -> none  [local(): jnp.concatenate([(pairs - base).reshape(-1), counts, lax.dynamic_slice_in...]
where the time goes in v2:
time: 48.9 us; the launch traced here: 48.7 us
  Pallas kernels  45.3 us (93%)
  between operations  1.41 us (3%)
  local copies, waits for them, and re-layouts  1.13 us (2%)
  other arithmetic  0.89 us (2%)
    pallas_call x1, Pallas kernels, direct_pairs(): pl.pallas_call(functools.partial(direct_kernel, n_row, n_col, REMOTE, LOC...  45.3 us

profile of v2, /device:TPU:1, one launch (start us, length us, event | category | flops | bytes accessed | tf_op | source)
XLA Modules:
  0.0 48.7 jit_solution(10815711574058245386)
XLA Ops:
  0.6 0.0 copy-start.2
  0.6 0.0 copy-start.3
  0.7 0.0 copy-start.1
  0.7 0.0 copy-start
  0.7 0.0 copy-start.6
  0.7 0.0 copy-start.5
  0.7 0.0 copy-start.4
  0.7 45.3 %shard_map.122 = (f32[4,32,1024]{2,1,0:T(8,128)S(1)}, f32[1,128]{1,0:T(1,128)S(1)}) custom-call(s32[4,2,16]{2,1,0:T(2,128)} %bitcast.10, s32[16]{0:T(128)} %counts.1, s32[3,512]{1,0:T(4,128)} %bitcast.9, f32[4,32,1024]{2,1,0:T(8,128)} %orb_hbm.1, f32[4,32,1024]{2,1,0:T(8,128)} %grad_hbm.1, bf16[2,1024,1024]{2,1,0:T(8,128)(2,1)} %constant.27.clone.kron_hbm, ...), custom_call_target="tpu_custom_call" | custom-call | tf_op jit(solution)/shard_map/pallas_call | solution.py:683
  46.0 0.6 %slice.6 = f32[1,1]{1,0:T(1,128)} slice(f32[1,128]{1,0:T(1,128)S(1)} %get-tuple-element.42), slice={[0:1], [2:3]} | slice | bytes 8 | tf_op jit(solution)/shard_map/slice | solution.py:740
  47.2 0.0 copy-done.2
  47.2 0.0 copy-done.3
  47.2 0.0 copy-done.1
  47.2 0.0 copy-done
  47.3 0.0 copy-done.6
  47.3 0.0 copy-done.5
  47.3 0.0 copy-done.4
  47.3 0.9 %subtract_subtract_fusion = f32[4,32,1024]{2,1,0:T(8,128)} fusion(f32[4,32,1024]{2,1,0:T(8,128)S(1)} %get-tuple-element.45, f32[4,32,1024]{2,1,0:T(8,128)S(1)} %get-tuple-element.46, f32[4,32,1024]{2,1,0:T(8,128)S(1)} %get-tuple-element.47), kind=kLoop, calls=%fused_computation.4 | loop fusion | flops 393216 | bytes 2097152 | tf_op jit(solution)/shard_map/cond/branch_0_fun/sub | solution.py:735
  48.2 0.5 %copy.21 = f32[2]{0:T(128)} copy(f32[2]{0:T(128)S(1)} %get-tuple-element.75) | data formatting | bytes 16
  (2 shorter events, 0.0 us)
Async XLA Ops:
  0.6 46.6 %copy-start.2 = (f32[32,1024]{1,0:T(8,128)S(1)}, f32[32,1024]{1,0:T(8,128)}, u32[]{:S(2)}) copy-start(f32[32,1024]{1,0:T(8,128)} %constant.29.clone.poly_hbm) | copy-start | bytes 393220
  0.6 46.6 %copy-start.3 = (bf16[2,128,128]{2,1,0:T(8,128)(2,1)S(1)}, bf16[2,128,128]{2,1,0:T(8,128)(2,1)}, u32[]{:S(2)}) copy-start(bf16[2,128,128]{2,1,0:T(8,128)(2,1)} %constant.30.clone) | copy-start | bytes 196612
  0.7 46.6 %copy-start.1 = (f32[4,32,1024]{2,1,0:T(8,128)S(1)}, f32[4,32,1024]{2,1,0:T(8,128)}, u32[]{:S(2)}) copy-start(f32[4,32,1024]{2,1,0:T(8,128)} %grad_hbm.1) | copy-start | bytes 1572868
  0.7 46.6 %copy-start = (f32[4,32,1024]{2,1,0:T(8,128)S(1)}, f32[4,32,1024]{2,1,0:T(8,128)}, u32[]{:S(2)}) copy-start(f32[4,32,1024]{2,1,0:T(8,128)} %orb_hbm.1) | copy-start | bytes 1572868
  0.7 46.6 %copy-start.6 = (s32[16]{0:T(128)S(1)}, s32[16]{0:T(128)}, u32[]{:S(2)}) copy-start(s32[16]{0:T(128)} %counts.1) | copy-start | bytes 196
  0.7 46.6 %copy-start.5 = (s32[16,4,2]{0,2,1:T(2,128)S(1)}, s32[16,4,2]{0,2,1:T(2,128)}, u32[]{:S(2)}) copy-start(s32[16,4,2]{0,2,1:T(2,128)} %param.16) | copy-start | bytes 1540
  0.7 46.6 %copy-start.4 = (s32[512,3]{0,1:T(4,128)S(1)}, s32[512,3]{0,1:T(4,128)}, u32[]{:S(2)}) copy-start(s32[512,3]{0,1:T(4,128)} %param.15) | copy-start | bytes 18436

commit v3 on v2

--- a/solution.py
+++ b/solution.py
@@ -391,14 +391,43 @@
     return updated, energies
 
 
+def flipped(x, edge):
+    per_tile = TILE_C // edge
+    tiles = x.shape[1] // TILE_C
+    block = lax.broadcasted_iota(jnp.int32, (1, TILE_C), 1) // edge
+    out = []
+    for t in reversed(range(tiles)):
+        tile = x[:, t * TILE_C : (t + 1) * TILE_C]
+        step = per_tile // 2
+        while step:
+            back = pltpu.roll(tile, TILE_C - step * edge, 1)
+            if 2 * step == per_tile:
+                tile = back
+            else:
+                ahead = pltpu.roll(tile, step * edge, 1)
+                tile = jnp.where(block // step % 2 == 0, back, ahead)
+            step //= 2
+        out.append(tile)
+    return jnp.concatenate(out, 1)
+
+
+def folded(basis, poly):
+    edge = basis.shape[0]
+    half = [np.kron(basis[i::2, : edge // 2].T, basis) for i in range(2)]
+    kron = np.stack([two_parts(x) for x in half + [x.T for x in half]])
+    poly = poly.reshape(edge, edge, edge)
+    poly = np.concatenate([poly[:, 0::2], poly[:, 1::2]], 1)
+    return kron, poly.reshape(edge, edge * edge)
+
+
 def direct_kernel(
     n_row,
     n_col,
     REMOTE,
     LOCAL,
-    pairs,
-    counts,
-    offsets,
+    pairs_hbm,
+    counts_hbm,
+    offsets_hbm,
     orb_hbm,
     grad_hbm,
     kron_hbm,
@@ -406,6 +435,10 @@
     poly_hbm,
     exchanged,
     energy_out,
+    over_out,
+    pairs,
+    counts,
+    offsets,
     orb,
     grad,
     kron,
@@ -440,15 +473,6 @@
     mesh_id = pl.DeviceIdType.MESH
     box_stage, slab = (stage0, stage1), (slab0, slab1)
 
-    loads = [
-        pltpu.make_async_copy(a, b, load_sem.at[i])
-        for i, (a, b) in enumerate(
-            ((orb_hbm, orb), (grad_hbm, grad), (kron_hbm, kron), (sx_hbm, sx), (poly_hbm, poly))
-        )
-    ]
-    for one in loads:
-        one.start()
-
     barrier = pltpu.get_barrier_semaphore()
     side, steps = peers(n_col)
 
@@ -463,6 +487,16 @@
         return 0
 
     lax.fori_loop(1, n_row, greet_row, 0)
+
+    sources = (pairs_hbm, counts_hbm, offsets_hbm, orb_hbm, grad_hbm, kron_hbm, sx_hbm, poly_hbm)
+    loads = [
+        pltpu.make_async_copy(a, b, load_sem.at[i])
+        for i, (a, b) in enumerate(zip(sources, (pairs, counts, offsets, orb, grad, kron, sx, poly)))
+    ]
+    for one in loads[:4]:
+        one.start()
+    for one in loads[:3]:
+        one.wait()
 
     lane = lax.broadcasted_iota(jnp.int32, (8, TILE_C), 1)
 
@@ -540,8 +574,8 @@
         fill(me)
         pltpu.make_async_copy(pack.at[r, me], dst, recv_sem.at[2 * r + 1]).start()
 
-    line = lax.broadcasted_iota(jnp.int32, (edge, plane), 0)
-    cell = lax.broadcasted_iota(jnp.int32, (edge, plane), 1)
+    line = lax.broadcasted_iota(jnp.int32, (edge, 1), 0)
+    cell = lax.broadcasted_iota(jnp.int32, (1, plane), 1)
 
     def work(r, start, number, between=None):
         firsts = []
@@ -567,16 +601,25 @@
             at_x = line + dx
             at_y = cell // edge + dy
             at_z = cell % edge + dz
-            inside = (at_x >= 0) & (at_x < edge) & (at_y >= 0) & (at_y < edge) & (at_z >= 0) & (at_z < edge)
-            moved = jnp.where(inside, moved, 0.0)
+            inside_x = ((at_x >= 0) & (at_x < edge)).astype(jnp.float32)
+            inside_yz = ((at_y >= 0) & (at_y < edge) & (at_z >= 0) & (at_z < edge)).astype(jnp.float32)
+            moved = moved * inside_yz * inside_x
             partner[pl.ds(n * edge, edge), :] = moved
             density[pl.ds(n * edge, edge), :] = box_stage[r][mine].astype(jnp.float32) * moved
         rows = number * edge
 
-        def along_yz(x):
+        def halves(x, which):
             high, low = split(x)
-            both = dot(jnp.concatenate([high, low], 0), kron[0])
-            return both[:rows] + (both[rows:] + dot(high, kron[1]))
+            both = dot(jnp.concatenate([high, low], 0), kron[which, 0])
+            return both[:rows] + (both[rows:] + dot(high, kron[which, 1]))
+
+        def to_modes(x):
+            near, far = x[:, : plane // 2], flipped(x[:, plane // 2 :], edge)
+            return jnp.concatenate([halves(near + far, 0), halves(near - far, 1)], 1)
+
+        def to_cells(x):
+            even, odd = halves(x[:, : plane // 2], 2), halves(x[:, plane // 2 :], 3)
+            return jnp.concatenate([even + odd, flipped(even - odd, edge)], 1)
 
         def along_x(x):
             high, low = split(x)
@@ -584,7 +627,7 @@
             both = dot(jnp.concatenate([part, sx[1, pl.ds(0, rows), pl.ds(0, rows)]], 0), high)
             return both[:rows] + (both[rows:] + dot(part, low))
 
-        modes = along_x(along_yz(density[pl.ds(0, rows), :])).reshape(number, edge, plane)
+        modes = along_x(to_modes(density[pl.ds(0, rows), :])).reshape(number, edge, plane)
         scaled = modes * poly[...][None]
         energy = jnp.zeros((8, TILE_C), jnp.float32)
         for n in range(number):
@@ -593,7 +636,7 @@
             energy = energy + jnp.where(firsts[n] >= 0, part, 0.0)
         if between is not None:
             between(energy)
-        potential = along_yz(along_x(scaled.reshape(rows, plane)))
+        potential = to_cells(along_x(scaled.reshape(rows, plane)))
         terms = (potential * partner[pl.ds(0, rows), :]).astype(jnp.bfloat16).astype(jnp.float32)
         for o in range(own):
             total = exchanged[o]
@@ -603,12 +646,14 @@
         return energy
 
     exchanged[...] = jnp.zeros_like(exchanged)
-    loads[0].wait()
+    loads[3].wait()
+    for one in loads[4:]:
+        one.start()
     box_stage[0][...] = orb[...].astype(jnp.bfloat16)
     pl.semaphore_wait(barrier, n_col - 1 + n_row - 1)
     send_boxes(0)
     to_scalars.wait()
-    for one in loads[1:]:
+    for one in loads[4:]:
         one.wait()
 
     def total_of(energy):
@@ -664,7 +709,11 @@
         sent(pack.at[r, pl.ds(0, others)], 2 * r + 1)
     sent(e_group.at[pl.ds(0, others)], 2 * ROUNDS)
     arrived(e_row, last)
-    energy_out[...] = jnp.sum(e_row[...], axis=0) / (edge * edge * edge * n_row * n_col)
+    values = jnp.sum(e_row[...], axis=0)
+    at = lax.broadcasted_iota(jnp.int32, (1, TILE_C), 1)
+    for i in range(ROUNDS):
+        energy_out[i] = jnp.sum(jnp.where(at == i, values, 0.0)) / (edge * edge * edge * n_row * n_col)
+    over_out[0] = jnp.sum(jnp.where(at == ROUNDS, values, 0.0))
     if n_row > 1:
         sent(e_row.at[pl.ds(0, n_row - 1)], last)
 
@@ -673,10 +722,9 @@
     own, edge, plane = orbitals.shape
     norb = own * n_col
     basis, poly = spectral_tables(edge)
-    kron = two_parts(np.kron(basis, basis))
+    kron, poly = folded(basis, poly)
     most = max(REMOTE, LOCAL - LOCAL // 2)
     sx = two_parts(np.kron(np.eye(most), basis))
-    hbm = pl.BlockSpec(memory_space=pltpu.HBM)
     smem = pl.BlockSpec(memory_space=pltpu.SMEM)
     vmem = pl.BlockSpec(memory_space=pltpu.VMEM)
     f32, bf16 = jnp.float32, jnp.bfloat16
@@ -684,14 +732,18 @@
         functools.partial(direct_kernel, n_row, n_col, REMOTE, LOCAL),
         out_shape=(
             jax.ShapeDtypeStruct((own, edge, plane), f32),
-            jax.ShapeDtypeStruct((1, TILE_C), f32),
+            jax.ShapeDtypeStruct((ROUNDS,), f32),
+            jax.ShapeDtypeStruct((1,), f32),
         ),
-        in_specs=[smem] * 3 + [hbm] * 5,
-        out_specs=(vmem, vmem),
+        in_specs=[pl.BlockSpec(memory_space=pl.ANY)] * 8,
+        out_specs=(vmem, smem, smem),
         scratch_shapes=[
+            pltpu.SMEM((pairs.shape[1], 2, n_col), jnp.int32),
+            pltpu.SMEM((n_col,), jnp.int32),
+            pltpu.SMEM((3, offsets.shape[0]), jnp.int32),
             pltpu.VMEM((own, edge, plane), f32),
             pltpu.VMEM((own, edge, plane), f32),
-            pltpu.VMEM((2, plane, plane), bf16),
+            pltpu.VMEM((4, 2, plane // 2, plane // 2), bf16),
             pltpu.VMEM((2, most * edge, most * edge), bf16),
             pltpu.VMEM((edge, plane), f32),
             pltpu.VMEM((own, edge, plane), bf16),
@@ -708,7 +760,7 @@
             pltpu.VMEM((n_row, 1, TILE_C), f32),
             pltpu.VMEM((16, TILE_C), jnp.int32),
             pltpu.SMEM((16, TILE_C), jnp.int32),
-            pltpu.SemaphoreType.DMA((5,)),
+            pltpu.SemaphoreType.DMA((8,)),
             pltpu.SemaphoreType.DMA((1,)),
             pltpu.SemaphoreType.DMA((2 * ROUNDS + 2,)),
             pltpu.SemaphoreType.DMA((2 * ROUNDS + 2,)),
@@ -729,15 +781,15 @@
 
 
 def local(n_row, n_col, REMOTE, LOCAL, S, orbitals, gradient, offsets, pairs, counts):
-    exchanged, values = direct_pairs(n_row, n_col, REMOTE, LOCAL, orbitals, gradient, offsets, pairs, counts)
+    exchanged, energies, over = direct_pairs(n_row, n_col, REMOTE, LOCAL, orbitals, gradient, offsets, pairs, counts)
 
     def enough():
-        return orbitals - gradient - damping * exchanged, values[0, :ROUNDS]
+        return orbitals - gradient - damping * exchanged, energies
 
     def general():
         return spread_pairs(n_row, n_col, S, orbitals, gradient, offsets, pairs, counts)
 
-    return lax.cond(values[0, ROUNDS] > 0, general, enough)
+    return lax.cond(over[0] > 0, general, enough)
 
 
 def solution(mesh):

time: 48.9 us -> 46.7 us (0.955)
  Pallas kernels: 45.3 us -> 43.5 us
  local copies, waits for them, and re-layouts: 1.13 us -> 0.55 us
    pallas_call x1, Pallas kernels: 45.3 us -> 43.5 us  [direct_pairs(): pl.pallas_call(functools.partial(direct_kernel, n_row, n_col, REMOTE, LOC...]
    slice x1 -> x0, local copies, waits for them, and re-layouts: 0.58 us -> none  [local(): return lax.cond(values[0, ROUNDS] > 0, general, enough)]
where the time goes in v3:
time: 46.7 us; the launch traced here: 46.6 us
  Pallas kernels  43.5 us (93%)
  between operations  1.38 us (3%)
  other arithmetic  0.89 us (2%)
  local copies, waits for them, and re-layouts  0.55 us (1%)
    pallas_call x1, Pallas kernels, direct_pairs(): pl.pallas_call(functools.partial(direct_kernel, n_row, n_col, REMOTE, LOC...  43.5 us

profile of v3, /device:TPU:1, one launch (start us, length us, event | category | flops | bytes accessed | tf_op | source)
XLA Modules:
  0.0 46.6 jit_solution(13606662757444469643)
XLA Ops:
  0.6 0.0 copy-start.2
  0.6 0.0 copy-start.3
  0.7 0.0 copy-start.1
  0.7 0.0 copy-start
  0.7 0.0 copy-start.6
  0.7 0.0 copy-start.5
  0.7 0.0 copy-start.4
  0.7 43.5 %shard_map.122 = (f32[4,32,1024]{2,1,0:T(8,128)S(1)}, f32[2]{0:T(128)S(1)}, f32[1]{0:T(128)}) custom-call(s32[4,2,16]{2,1,0:T(2,128)} %bitcast.8, s32[16]{0:T(128)} %counts_hbm.1, s32[3,512]{1,0:T(4,128)} %bitcast.7, f32[4,32,1024]{2,1,0:T(8,128)} %orb_hbm.1, f32[4,32,1024]{2,1,0:T(8,128)} %grad_hbm.1, bf16[4,2,512,512]{3,2,1,0:T(8,128)(2,1)} %constant.31.clone.kron_hbm, ...), custom_call_target="tpu_custom_call" | custom-call | tf_op jit(solution)/shard_map/pallas_call | solution.py:731
  44.9 0.0 copy-done.2
  44.9 0.0 copy-done.3
  44.9 0.0 copy-done.1
  44.9 0.0 copy-done
  44.9 0.0 copy-done.6
  44.9 0.0 copy-done.5
  44.9 0.0 copy-done.4
  44.9 0.2 conditional.1
  45.2 0.9 %subtract_subtract_fusion = f32[4,32,1024]{2,1,0:T(8,128)} fusion(f32[4,32,1024]{2,1,0:T(8,128)S(1)} %get-tuple-element.47, f32[4,32,1024]{2,1,0:T(8,128)S(1)} %get-tuple-element.48, f32[4,32,1024]{2,1,0:T(8,128)S(1)} %get-tuple-element.49), kind=kLoop, calls=%fused_computation.3 | loop fusion | flops 393216 | bytes 2097152 | tf_op jit(solution)/shard_map/cond/branch_0_fun/sub | solution.py:787
  46.1 0.5 %copy.21 = f32[2]{0:T(128)} copy(f32[2]{0:T(128)S(1)} %get-tuple-element.77) | data formatting | bytes 16
Async XLA Ops:
  0.6 44.2 %copy-start.2 = (f32[32,1024]{1,0:T(8,128)S(1)}, f32[32,1024]{1,0:T(8,128)}, u32[]{:S(2)}) copy-start(f32[32,1024]{1,0:T(8,128)} %constant.36.clone) | copy-start | bytes 393220
  0.6 44.2 %copy-start.3 = (bf16[2,128,128]{2,1,0:T(8,128)(2,1)S(1)}, bf16[2,128,128]{2,1,0:T(8,128)(2,1)}, u32[]{:S(2)}) copy-start(bf16[2,128,128]{2,1,0:T(8,128)(2,1)} %constant.35.clone) | copy-start | bytes 196612
  0.7 44.2 %copy-start.1 = (f32[4,32,1024]{2,1,0:T(8,128)S(1)}, f32[4,32,1024]{2,1,0:T(8,128)}, u32[]{:S(2)}) copy-start(f32[4,32,1024]{2,1,0:T(8,128)} %grad_hbm.1) | copy-start | bytes 1572868
  0.7 44.2 %copy-start = (f32[4,32,1024]{2,1,0:T(8,128)S(1)}, f32[4,32,1024]{2,1,0:T(8,128)}, u32[]{:S(2)}) copy-start(f32[4,32,1024]{2,1,0:T(8,128)} %orb_hbm.1) | copy-start | bytes 1572868
  0.7 44.2 %copy-start.6 = (s32[16]{0:T(128)S(1)}, s32[16]{0:T(128)}, u32[]{:S(2)}) copy-start(s32[16]{0:T(128)} %counts_hbm.1) | copy-start | bytes 196
  0.7 44.2 %copy-start.5 = (s32[16,4,2]{0,2,1:T(2,128)S(1)}, s32[16,4,2]{0,2,1:T(2,128)}, u32[]{:S(2)}) copy-start(s32[16,4,2]{0,2,1:T(2,128)} %param.16) | copy-start | bytes 1540
  0.7 44.2 %copy-start.4 = (s32[512,3]{0,1:T(4,128)S(1)}, s32[512,3]{0,1:T(4,128)}, u32[]{:S(2)}) copy-start(s32[512,3]{0,1:T(4,128)} %param.15) | copy-start | bytes 18436

commit v4 on v3

--- a/solution.py
+++ b/solution.py
@@ -420,6 +420,24 @@
     return kron, poly.reshape(edge, edge * edge)
 
 
+def along_lanes(x, step):
+    tiles = x.shape[1] // TILE_C
+    left = step < 0
+    turn = jnp.where(left, step + TILE_C, step)
+    lane = lax.broadcasted_iota(jnp.int32, (1, TILE_C), 1)
+    own = lane < TILE_C - turn
+    back = lax.rem(TILE_C - turn, jnp.int32(TILE_C))
+    turned = [pltpu.roll(x[:, t * TILE_C : (t + 1) * TILE_C], back, 1) for t in range(tiles)]
+    before = own & left
+    after = jnp.logical_not(own | left)
+    out = []
+    for t in range(tiles):
+        tile = turned[t]
+        tile = jnp.where(before, turned[t - 1], tile) if t > 0 else tile
+        out.append(jnp.where(after, turned[t + 1], tile) if t < tiles - 1 else tile)
+    return jnp.concatenate(out, 1)
+
+
 def direct_kernel(
     n_row,
     n_col,
@@ -433,9 +451,10 @@
     kron_hbm,
     sx_hbm,
     poly_hbm,
-    exchanged,
+    updated_hbm,
     energy_out,
     over_out,
+    exchanged,
     pairs,
     counts,
     offsets,
@@ -596,7 +615,7 @@
             else:
                 moved = box_stage[r][jnp.clip(second - base - me * own, 0, own - 1)]
             moved = moved.astype(jnp.float32)
-            moved = pltpu.roll(moved, lax.rem(plane - t, jnp.int32(plane)), 1)
+            moved = along_lanes(moved, t)
             moved = pltpu.roll(moved, lax.rem(edge - dx, jnp.int32(edge)), 0)
             at_x = line + dx
             at_y = cell // edge + dy
@@ -627,15 +646,25 @@
             both = dot(jnp.concatenate([part, sx[1, pl.ds(0, rows), pl.ds(0, rows)]], 0), high)
             return both[:rows] + (both[rows:] + dot(part, low))
 
+        def energy_of(modes, scaled):
+            energy = jnp.zeros((8, TILE_C), jnp.float32)
+            for n in range(number):
+                part = jnp.sum((modes[n] * scaled[n]).reshape(edge // 8, 8, plane), axis=0)
+                part = sum(part[:, c * TILE_C : (c + 1) * TILE_C] for c in range(strips))
+                energy = energy + jnp.where(firsts[n] >= 0, part, 0.0)
+            return energy
+
+        if between is not None:
+            x = density[pl.ds(0, rows), :]
+            near, far = x[:, : plane // 2], flipped(x[:, plane // 2 :], edge)
+            modes = jnp.concatenate(
+                [dot(y.astype(jnp.bfloat16), kron[i, 0]).astype(jnp.bfloat16) for i, y in enumerate((near + far, near - far))], 1
+            )
+            modes = dot(sx[0, pl.ds(0, rows), pl.ds(0, rows)], modes).reshape(number, edge, plane)
+            between(energy_of(modes, modes * poly[...][None]))
         modes = along_x(to_modes(density[pl.ds(0, rows), :])).reshape(number, edge, plane)
         scaled = modes * poly[...][None]
-        energy = jnp.zeros((8, TILE_C), jnp.float32)
-        for n in range(number):
-            part = jnp.sum((modes[n] * scaled[n]).reshape(edge // 8, 8, plane), axis=0)
-            part = sum(part[:, c * TILE_C : (c + 1) * TILE_C] for c in range(strips))
-            energy = energy + jnp.where(firsts[n] >= 0, part, 0.0)
-        if between is not None:
-            between(energy)
+        energy = energy_of(modes, scaled) if between is None else None
         potential = to_cells(along_x(scaled.reshape(rows, plane)))
         terms = (potential * partner[pl.ds(0, rows), :]).astype(jnp.bfloat16).astype(jnp.float32)
         for o in range(own):
@@ -686,6 +715,10 @@
 
             work(r, 0, REMOTE, send_energy)
 
+    orb[...] = orb[...] - damping * (ROUNDS * grad[...] + exchanged[...])
+    store = pltpu.make_async_copy(orb, updated_hbm, slot_sem.at[0])
+    store.start()
+
     arrived(e_group, 2 * ROUNDS)
     e_sum[...] = jnp.sum(e_group[...], axis=0)
     last = 2 * ROUNDS + 1
@@ -708,6 +741,7 @@
         sent(slab[r].at[pl.ds(0, others * own)], 2 * r)
         sent(pack.at[r, pl.ds(0, others)], 2 * r + 1)
     sent(e_group.at[pl.ds(0, others)], 2 * ROUNDS)
+    store.wait()
     arrived(e_row, last)
     values = jnp.sum(e_row[...], axis=0)
     at = lax.broadcasted_iota(jnp.int32, (1, TILE_C), 1)
@@ -726,7 +760,6 @@
     most = max(REMOTE, LOCAL - LOCAL // 2)
     sx = two_parts(np.kron(np.eye(most), basis))
     smem = pl.BlockSpec(memory_space=pltpu.SMEM)
-    vmem = pl.BlockSpec(memory_space=pltpu.VMEM)
     f32, bf16 = jnp.float32, jnp.bfloat16
     return pl.pallas_call(
         functools.partial(direct_kernel, n_row, n_col, REMOTE, LOCAL),
@@ -736,8 +769,9 @@
             jax.ShapeDtypeStruct((1,), f32),
         ),
         in_specs=[pl.BlockSpec(memory_space=pl.ANY)] * 8,
-        out_specs=(vmem, smem, smem),
+        out_specs=(pl.BlockSpec(memory_space=pl.ANY), smem, smem),
         scratch_shapes=[
+            pltpu.VMEM((own, edge, plane), f32),
             pltpu.SMEM((pairs.shape[1], 2, n_col), jnp.int32),
             pltpu.SMEM((n_col,), jnp.int32),
             pltpu.SMEM((3, offsets.shape[0]), jnp.int32),
@@ -781,10 +815,10 @@
 
 
 def local(n_row, n_col, REMOTE, LOCAL, S, orbitals, gradient, offsets, pairs, counts):
-    exchanged, energies, over = direct_pairs(n_row, n_col, REMOTE, LOCAL, orbitals, gradient, offsets, pairs, counts)
+    updated, energies, over = direct_pairs(n_row, n_col, REMOTE, LOCAL, orbitals, gradient, offsets, pairs, counts)
 
     def enough():
-        return orbitals - gradient - damping * exchanged, energies
+        return updated, energies
 
     def general():
         return spread_pairs(n_row, n_col, S, orbitals, gradient, offsets, pairs, counts)

time: 46.7 us -> 46 us (0.985)
  other arithmetic: 0.89 us -> 0 us
  local copies, waits for them, and re-layouts: 0.55 us -> 1.33 us
  Pallas kernels: 43.5 us -> 42.9 us
    sub x1 -> x0, other arithmetic: 0.89 us -> none  [enough(): return (orbitals - gradient - damping * exchanged, energies)]
    unnamed x15 -> x12, local copies, waits for them, and re-layouts: 0.55 us -> 1.33 us
    pallas_call x1, Pallas kernels: 43.5 us -> 42.9 us  [direct_pairs(): pl.pallas_call(functools.partial(direct_kernel, n_row, n_col, REMOTE, LOC...]
where the time goes in v4:
time: 46 us; the launch traced here: 45.8 us
  Pallas kernels  42.9 us (93%)
  between operations  1.35 us (3%)
  local copies, waits for them, and re-layouts  1.33 us (3%)
    pallas_call x1, Pallas kernels, direct_pairs(): pl.pallas_call(functools.partial(direct_kernel, n_row, n_col, REMOTE, LOC...  42.9 us
    unnamed x12, local copies, waits for them, and re-layouts  1.33 us

profile of v4, /device:TPU:1, one launch (start us, length us, event | category | flops | bytes accessed | tf_op | source)
XLA Modules:
  0.0 45.8 jit_solution(2179168365336001982)
XLA Ops:
  0.6 0.0 copy-start.4
  0.6 0.0 copy-start.3
  0.7 0.0 copy-start.2
  0.7 0.0 copy-start.1
  0.7 0.0 copy-start
  0.7 42.9 %shard_map.134 = (f32[4,32,1024]{2,1,0:T(8,128)S(1)}, f32[2]{0:T(128)S(1)}, f32[1]{0:T(128)}) custom-call(s32[4,2,16]{2,1,0:T(2,128)} %bitcast.8, s32[16]{0:T(128)} %counts_hbm.1, s32[3,512]{1,0:T(4,128)} %bitcast.7, f32[4,32,1024]{2,1,0:T(8,128)} %orb_hbm.1, f32[4,32,1024]{2,1,0:T(8,128)} %grad_hbm.1, bf16[4,2,512,512]{3,2,1,0:T(8,128)(2,1)} %constant.29.clone.kron_hbm, ...), custom_call_target="tpu_custom_call" | custom-call | tf_op jit(solution)/shard_map/pallas_call | solution.py:764
  44.2 0.0 copy-done.4
  44.3 0.0 copy-done.3
  44.3 0.0 copy-done.2
  44.3 0.0 copy-done.1
  44.3 0.0 copy-done
  44.3 0.2 conditional.1
  44.5 0.8 %copy.34 = f32[4,32,1024]{2,1,0:T(8,128)} copy(f32[4,32,1024]{2,1,0:T(8,128)S(1)} %get-tuple-element.76) | data formatting | bytes 1048576
  45.3 0.5 %copy.35 = f32[2]{0:T(128)} copy(f32[2]{0:T(128)S(1)} %get-tuple-element.77) | data formatting | bytes 16
Async XLA Ops:
  0.6 43.6 %copy-start.4 = (s32[16]{0:T(128)S(1)}, s32[16]{0:T(128)}, u32[]{:S(2)}) copy-start(s32[16]{0:T(128)} %counts_hbm.1) | copy-start | bytes 196
  0.6 43.6 %copy-start.3 = (s32[16,4,2]{0,2,1:T(2,128)S(1)}, s32[16,4,2]{0,2,1:T(2,128)}, u32[]{:S(2)}) copy-start(s32[16,4,2]{0,2,1:T(2,128)} %param.16) | copy-start | bytes 1540
  0.7 43.6 %copy-start.2 = (s32[512,3]{0,1:T(4,128)S(1)}, s32[512,3]{0,1:T(4,128)}, u32[]{:S(2)}) copy-start(s32[512,3]{0,1:T(4,128)} %param.15) | copy-start | bytes 18436
  0.7 43.6 %copy-start.1 = (f32[4,32,1024]{2,1,0:T(8,128)S(1)}, f32[4,32,1024]{2,1,0:T(8,128)}, u32[]{:S(2)}) copy-start(f32[4,32,1024]{2,1,0:T(8,128)} %grad_hbm.1) | copy-start | bytes 1572868
  0.7 43.6 %copy-start = (f32[4,32,1024]{2,1,0:T(8,128)S(1)}, f32[4,32,1024]{2,1,0:T(8,128)}, u32[]{:S(2)}) copy-start(f32[4,32,1024]{2,1,0:T(8,128)} %orb_hbm.1) | copy-start | bytes 1572868

commit v5 on v4

--- a/solution.py
+++ b/solution.py
@@ -641,10 +641,11 @@
             return jnp.concatenate([even + odd, flipped(even - odd, edge)], 1)
 
         def along_x(x):
-            high, low = split(x)
-            part = sx[0, pl.ds(0, rows), pl.ds(0, rows)]
-            both = dot(jnp.concatenate([part, sx[1, pl.ds(0, rows), pl.ds(0, rows)]], 0), high)
-            return both[:rows] + (both[rows:] + dot(part, low))
+            out = []
+            for n in range(number):
+                high, low = split(x[n * edge : (n + 1) * edge])
+                out.append(dot(sx[...], jnp.concatenate([high, low, high], 0)))
+            return jnp.concatenate(out, 0)
 
         def energy_of(modes, scaled):
             energy = jnp.zeros((8, TILE_C), jnp.float32)
@@ -660,7 +661,8 @@
             modes = jnp.concatenate(
                 [dot(y.astype(jnp.bfloat16), kron[i, 0]).astype(jnp.bfloat16) for i, y in enumerate((near + far, near - far))], 1
             )
-            modes = dot(sx[0, pl.ds(0, rows), pl.ds(0, rows)], modes).reshape(number, edge, plane)
+            part = sx[...][:, :edge]
+            modes = jnp.stack([dot(part, modes[n * edge : (n + 1) * edge]) for n in range(number)])
             between(energy_of(modes, modes * poly[...][None]))
         modes = along_x(to_modes(density[pl.ds(0, rows), :])).reshape(number, edge, plane)
         scaled = modes * poly[...][None]
@@ -758,7 +760,8 @@
     basis, poly = spectral_tables(edge)
     kron, poly = folded(basis, poly)
     most = max(REMOTE, LOCAL - LOCAL // 2)
-    sx = two_parts(np.kron(np.eye(most), basis))
+    high, low = two_parts(basis)
+    sx = np.concatenate([high, high, low], 1)
     smem = pl.BlockSpec(memory_space=pltpu.SMEM)
     f32, bf16 = jnp.float32, jnp.bfloat16
     return pl.pallas_call(
@@ -778,7 +781,7 @@
             pltpu.VMEM((own, edge, plane), f32),
             pltpu.VMEM((own, edge, plane), f32),
             pltpu.VMEM((4, 2, plane // 2, plane // 2), bf16),
-            pltpu.VMEM((2, most * edge, most * edge), bf16),
+            pltpu.VMEM((edge, 3 * edge), bf16),
             pltpu.VMEM((edge, plane), f32),
             pltpu.VMEM((own, edge, plane), bf16),
             pltpu.VMEM((own, edge, plane), bf16),

time: 46 us -> 45.7 us (level)
  no operation moved by 1% of the time
where the time goes in v5:
time: 45.7 us; the launch traced here: 45.6 us
  Pallas kernels  42.7 us (93%)
  between operations  1.35 us (3%)
  local copies, waits for them, and re-layouts  1.33 us (3%)
    pallas_call x1, Pallas kernels, direct_pairs(): pl.pallas_call(functools.partial(direct_kernel, n_row, n_col, REMOTE, LOC...  42.7 us
    unnamed x12, local copies, waits for them, and re-layouts  1.33 us

profile of v5, /device:TPU:1, one launch (start us, length us, event | category | flops | bytes accessed | tf_op | source)
XLA Modules:
  0.0 45.6 jit_solution(14058668689615220224)
XLA Ops:
  0.6 0.0 copy-start.4
  0.6 0.0 copy-start.3
  0.7 0.0 copy-start.2
  0.7 0.0 copy-start.1
  0.7 0.0 copy-start
  0.7 42.7 %shard_map.134 = (f32[4,32,1024]{2,1,0:T(8,128)S(1)}, f32[2]{0:T(128)S(1)}, f32[1]{0:T(128)}) custom-call(s32[4,2,16]{2,1,0:T(2,128)} %bitcast.8, s32[16]{0:T(128)} %counts_hbm.1, s32[3,512]{1,0:T(4,128)} %bitcast.7, f32[4,32,1024]{2,1,0:T(8,128)} %orb_hbm.1, f32[4,32,1024]{2,1,0:T(8,128)} %grad_hbm.1, bf16[4,2,512,512]{3,2,1,0:T(8,128)(2,1)} %constant.29.clone.kron_hbm, ...), custom_call_target="tpu_custom_call" | custom-call | tf_op jit(solution)/shard_map/pallas_call | solution.py:767
  44.0 0.0 copy-done.4
  44.0 0.0 copy-done.3
  44.0 0.0 copy-done.2
  44.0 0.0 copy-done.1
  44.0 0.0 copy-done
  44.1 0.2 conditional.1
  44.2 0.8 %copy.34 = f32[4,32,1024]{2,1,0:T(8,128)} copy(f32[4,32,1024]{2,1,0:T(8,128)S(1)} %get-tuple-element.76) | data formatting | bytes 1048576
  45.0 0.5 %copy.35 = f32[2]{0:T(128)} copy(f32[2]{0:T(128)S(1)} %get-tuple-element.77) | data formatting | bytes 16
Async XLA Ops:
  0.6 43.4 %copy-start.4 = (s32[16]{0:T(128)S(1)}, s32[16]{0:T(128)}, u32[]{:S(2)}) copy-start(s32[16]{0:T(128)} %counts_hbm.1) | copy-start | bytes 196
  0.6 43.4 %copy-start.3 = (s32[16,4,2]{0,2,1:T(2,128)S(1)}, s32[16,4,2]{0,2,1:T(2,128)}, u32[]{:S(2)}) copy-start(s32[16,4,2]{0,2,1:T(2,128)} %param.16) | copy-start | bytes 1540
  0.7 43.4 %copy-start.2 = (s32[512,3]{0,1:T(4,128)S(1)}, s32[512,3]{0,1:T(4,128)}, u32[]{:S(2)}) copy-start(s32[512,3]{0,1:T(4,128)} %param.15) | copy-start | bytes 18436
  0.7 43.4 %copy-start.1 = (f32[4,32,1024]{2,1,0:T(8,128)S(1)}, f32[4,32,1024]{2,1,0:T(8,128)}, u32[]{:S(2)}) copy-start(f32[4,32,1024]{2,1,0:T(8,128)} %grad_hbm.1) | copy-start | bytes 1572868
  0.7 43.4 %copy-start = (f32[4,32,1024]{2,1,0:T(8,128)S(1)}, f32[4,32,1024]{2,1,0:T(8,128)}, u32[]{:S(2)}) copy-start(f32[4,32,1024]{2,1,0:T(8,128)} %orb_hbm.1) | copy-start | bytes 1572868

commit v6 on v4

--- a/solution.py
+++ b/solution.py
@@ -477,6 +477,8 @@
     e_row,
     slot_rows,
     slot_of,
+    held,
+    inside_yz,
     load_sem,
     slot_sem,
     send_sem,
@@ -522,24 +524,28 @@
     def place(index, state):
         p, k = index // per_owner, index % per_owner
         at_first = lax.div(pairs[k, 0, p] - base, jnp.int32(own))
-        at_second = lax.div(pairs[k, 1, p] - base, jnp.int32(own))
+        second = jnp.clip(pairs[k, 1, p] - base, 0, norb - 1)
+        at_second = lax.div(second, jnp.int32(own))
         here = jnp.where(k < counts[p], at_first, -1)
         far = jnp.where(at_first == at_second, -1, here)
         near = jnp.where(at_first == at_second, here, -1)
-        out = []
-        for device, (count, slots) in zip((far, near), state):
-            hit = lane == device
-            slots = tuple(jnp.where(hit & (count == s), index, held) for s, held in enumerate(slots))
-            out.append((count + hit.astype(jnp.int32), slots))
-        return tuple(out)
+        far_count, far_slots, far_seconds, near_count, near_slots = state
+        hit = lane == far
+        here = [hit & (far_count == s) for s in range(REMOTE)]
+        far_slots = tuple(jnp.where(at, index, was) for at, was in zip(here, far_slots))
+        far_seconds = tuple(jnp.where(at, second, was) for at, was in zip(here, far_seconds))
+        far_count = far_count + hit.astype(jnp.int32)
+        hit = lane == near
+        near_slots = tuple(jnp.where(hit & (near_count == s), index, was) for s, was in enumerate(near_slots))
+        return far_count, far_slots, far_seconds, near_count + hit.astype(jnp.int32), near_slots
 
     none = jnp.full((8, TILE_C), -1, jnp.int32)
     zero = jnp.zeros((8, TILE_C), jnp.int32)
-    (far_count, far_slots), (near_count, near_slots) = lax.fori_loop(
-        0, n_col * per_owner, place, ((zero, (none,) * REMOTE), (zero, (none,) * LOCAL))
+    far_count, far_slots, far_seconds, near_count, near_slots = lax.fori_loop(
+        0, n_col * per_owner, place, (zero, (none,) * REMOTE, (zero,) * REMOTE, zero, (none,) * LOCAL)
     )
-    for s, held in enumerate(far_slots + near_slots):
-        slot_rows[pl.ds(s, 1), :] = held[0:1, :]
+    for s, entry in enumerate(far_slots + near_slots + far_seconds):
+        slot_rows[pl.ds(s, 1), :] = entry[0:1, :]
     over = ((far_count > REMOTE) | (near_count > LOCAL)).astype(jnp.float32)
     overflow = jnp.sum(over[0:1, :], axis=1, keepdims=True)
     to_scalars = pltpu.make_async_copy(slot_rows, slot_of, slot_sem.at[0])
@@ -583,9 +589,7 @@
 
         def fill(to):
             for s in range(REMOTE):
-                index = jnp.maximum(slot_of[s, to], 0)
-                second = pairs[lax.rem(index, jnp.int32(per_owner)), 1, lax.div(index, jnp.int32(per_owner))]
-                pack[r, to, s] = slab[r][jnp.clip(second - base, 0, norb - 1)]
+                pack[r, to, s] = slab[r][slot_of[REMOTE + LOCAL + s, to]]
 
         for step in steps:
             fill(peer(step))
@@ -599,30 +603,17 @@
     def work(r, start, number, between=None):
         firsts = []
         for n in range(number):
-            code = slot_of[start + n, me]
-            index = jnp.maximum(code, 0)
-            p = lax.div(index, jnp.int32(per_owner))
-            k = lax.rem(index, jnp.int32(per_owner))
-            first, second = pairs[k, 0, p], pairs[k, 1, p]
-            mine = jnp.clip(first - base - me * own, 0, own - 1)
-            firsts.append(jnp.where(code >= 0, mine, -1))
-            dx = offsets[0, first] - offsets[0, second]
-            dy = offsets[1, first] - offsets[1, second]
-            dz = offsets[2, first] - offsets[2, second]
-            t = dy * edge + dz
+            live, mine, other, t, dx = facts[start + n]
+            firsts.append(live)
             if start < REMOTE:
                 moved = pair_box[r, start + n]
             else:
-                moved = box_stage[r][jnp.clip(second - base - me * own, 0, own - 1)]
+                moved = box_stage[r][other]
             moved = moved.astype(jnp.float32)
             moved = along_lanes(moved, t)
             moved = pltpu.roll(moved, lax.rem(edge - dx, jnp.int32(edge)), 0)
-            at_x = line + dx
-            at_y = cell // edge + dy
-            at_z = cell % edge + dz
-            inside_x = ((at_x >= 0) & (at_x < edge)).astype(jnp.float32)
-            inside_yz = ((at_y >= 0) & (at_y < edge) & (at_z >= 0) & (at_z < edge)).astype(jnp.float32)
-            moved = moved * inside_yz * inside_x
+            inside_x = ((line + dx >= 0) & (line + dx < edge)).astype(jnp.float32)
+            moved = moved * inside_yz[start + n] * inside_x
             partner[pl.ds(n * edge, edge), :] = moved
             density[pl.ds(n * edge, edge), :] = box_stage[r][mine].astype(jnp.float32) * moved
         rows = number * edge
@@ -685,6 +676,23 @@
     for one in loads[4:]:
         one.wait()
 
+    facts = []
+    for slot in range(REMOTE + LOCAL):
+        code = slot_of[slot, me]
+        index = jnp.maximum(code, 0)
+        p, k = lax.div(index, jnp.int32(per_owner)), lax.rem(index, jnp.int32(per_owner))
+        first, second = pairs[k, 0, p], pairs[k, 1, p]
+        mine = jnp.clip(first - base - me * own, 0, own - 1)
+        other = jnp.clip(second - base - me * own, 0, own - 1)
+        dx = offsets[0, first] - offsets[0, second]
+        dy = offsets[1, first] - offsets[1, second]
+        dz = offsets[2, first] - offsets[2, second]
+        at_y, at_z = cell // edge + dy, cell % edge + dz
+        inside = (at_y >= 0) & (at_y < edge) & (at_z >= 0) & (at_z < edge)
+        inside_yz[slot] = inside.astype(jnp.float32)
+        facts.append((jnp.where(code >= 0, mine, -1), mine, other, dy * edge + dz, dx))
+    held[...] = orb[...] - damping * grad[...]
+
     def total_of(energy):
         return jnp.sum(jnp.sum(energy, axis=0, keepdims=True), axis=1, keepdims=True)
 
@@ -698,7 +706,7 @@
         arrived(pair_box.at[r], 2 * r + 1)
         if r < ROUNDS - 1:
             kept.append(total_of(energy + work(r, 0, REMOTE)))
-            box_stage[r + 1][...] = (orb[...] - damping * ((r + 1.0) * grad[...] + exchanged[...])).astype(jnp.bfloat16)
+            box_stage[r + 1][...] = (held[...] - damping * exchanged[...]).astype(jnp.bfloat16)
             send_boxes(r + 1)
         else:
 
@@ -792,8 +800,10 @@
             pltpu.VMEM((n_col, 1, TILE_C), f32),
             pltpu.VMEM((1, TILE_C), f32),
             pltpu.VMEM((n_row, 1, TILE_C), f32),
-            pltpu.VMEM((16, TILE_C), jnp.int32),
-            pltpu.SMEM((16, TILE_C), jnp.int32),
+            pltpu.VMEM((-(-(2 * REMOTE + LOCAL) // 8) * 8, TILE_C), jnp.int32),
+            pltpu.SMEM((-(-(2 * REMOTE + LOCAL) // 8) * 8, TILE_C), jnp.int32),
+            pltpu.VMEM((own, edge, plane), f32),
+            pltpu.VMEM((REMOTE + LOCAL, 1, plane), f32),
             pltpu.SemaphoreType.DMA((8,)),
             pltpu.SemaphoreType.DMA((1,)),
             pltpu.SemaphoreType.DMA((2 * ROUNDS + 2,)),

time: 46 us -> 46 us (level)
  no operation moved by 1% of the time
where the time goes in v6:
time: 46 us; the launch traced here: 45.9 us
  Pallas kernels  43 us (93%)
  between operations  1.35 us (3%)
  local copies, waits for them, and re-layouts  1.33 us (3%)
    pallas_call x1, Pallas kernels, direct_pairs(): pl.pallas_call(functools.partial(direct_kernel, n_row, n_col, REMOTE, LOC...  43 us
    unnamed x12, local copies, waits for them, and re-layouts  1.33 us

profile of v6, /device:TPU:1, one launch (start us, length us, event | category | flops | bytes accessed | tf_op | source)
XLA Modules:
  0.0 45.9 jit_solution(16005200016563846264)
XLA Ops:
  0.6 0.0 copy-start.4
  0.6 0.0 copy-start.3
  0.7 0.0 copy-start.2
  0.7 0.0 copy-start.1
  0.7 0.0 copy-start
  0.7 43.0 %shard_map.134 = (f32[4,32,1024]{2,1,0:T(8,128)S(1)}, f32[2]{0:T(128)S(1)}, f32[1]{0:T(128)}) custom-call(s32[4,2,16]{2,1,0:T(2,128)} %bitcast.8, s32[16]{0:T(128)} %counts_hbm.1, s32[3,512]{1,0:T(4,128)} %bitcast.7, f32[4,32,1024]{2,1,0:T(8,128)} %orb_hbm.1, f32[4,32,1024]{2,1,0:T(8,128)} %grad_hbm.1, bf16[4,2,512,512]{3,2,1,0:T(8,128)(2,1)} %constant.29.clone.kron_hbm, ...), custom_call_target="tpu_custom_call" | custom-call | tf_op jit(solution)/shard_map/pallas_call | solution.py:772
  44.3 0.0 copy-done.4
  44.3 0.0 copy-done.3
  44.4 0.0 copy-done.2
  44.4 0.0 copy-done.1
  44.4 0.0 copy-done
  44.4 0.2 conditional.1
  44.6 0.8 %copy.34 = f32[4,32,1024]{2,1,0:T(8,128)} copy(f32[4,32,1024]{2,1,0:T(8,128)S(1)} %get-tuple-element.76) | data formatting | bytes 1048576
  45.4 0.5 %copy.35 = f32[2]{0:T(128)} copy(f32[2]{0:T(128)S(1)} %get-tuple-element.77) | data formatting | bytes 16
Async XLA Ops:
  0.6 43.7 %copy-start.4 = (s32[16]{0:T(128)S(1)}, s32[16]{0:T(128)}, u32[]{:S(2)}) copy-start(s32[16]{0:T(128)} %counts_hbm.1) | copy-start | bytes 196
  0.6 43.7 %copy-start.3 = (s32[16,4,2]{0,2,1:T(2,128)S(1)}, s32[16,4,2]{0,2,1:T(2,128)}, u32[]{:S(2)}) copy-start(s32[16,4,2]{0,2,1:T(2,128)} %param.16) | copy-start | bytes 1540
  0.7 43.7 %copy-start.2 = (s32[512,3]{0,1:T(4,128)S(1)}, s32[512,3]{0,1:T(4,128)}, u32[]{:S(2)}) copy-start(s32[512,3]{0,1:T(4,128)} %param.15) | copy-start | bytes 18436
  0.7 43.7 %copy-start.1 = (f32[4,32,1024]{2,1,0:T(8,128)S(1)}, f32[4,32,1024]{2,1,0:T(8,128)}, u32[]{:S(2)}) copy-start(f32[4,32,1024]{2,1,0:T(8,128)} %grad_hbm.1) | copy-start | bytes 1572868
  0.7 43.7 %copy-start = (f32[4,32,1024]{2,1,0:T(8,128)S(1)}, f32[4,32,1024]{2,1,0:T(8,128)}, u32[]{:S(2)}) copy-start(f32[4,32,1024]{2,1,0:T(8,128)} %orb_hbm.1) | copy-start | bytes 1572868
